TPU v7x, 32 devices: a whole 2x2x4 slice. The times are simulated.
32 devices in a mesh: section: 4 (over y, x), row: 2 (over core), col: 4 (over z).
Axes of the slice: x: 2, y: 2, z: 4, core: 2. Of those that a mesh axis runs over, the one named last changes fastest.
Arguments:
- latent: bfloat16 [2, 32, 64, 128], P(None, 'row', 'col'), may hold values from -6 to 6
- hidden_old: bfloat16 [4, 2, 32, 64, 128], P('section', None, 'row', 'col'), may hold values from -1 to 1
- cell_old: float32 [4, 2, 32, 64, 128], P('section', None, 'row', 'col'), may hold values from -6 to 6
- weights: bfloat16 [4, 9, 256, 512], P('section'), may hold values from -0.125 to 0.125
- bias: float32 [4, 512], P('section'), may hold values from -3 to 3
Outputs:
- hidden_new: bfloat16 [4, 2, 32, 64, 128], P('section', None, 'row', 'col')
- cell_new: float32 [4, 2, 32, 64, 128], P('section', None, 'row', 'col')
All inputs are finite; a program needn't handle non-finite values.
Results may differ from a plain program's by a relative error of at most 0.0016.
Values may be sent and summed in bfloat16 or wider, within the bound.
A program may use at most 64 MiB of HBM per device.

v0:
```python
import jax
import jax.numpy as jnp
from jax import lax
from jax.sharding import PartitionSpec as P


def shifted(x, axis, by):
    length = lax.axis_size(axis)
    pairs = [(i, i + by) for i in range(length) if 0 <= i + by < length]
    return lax.ppermute(x, axis, pairs)


def padded_2(cells, sides, width):
    for axis, dim in sides:
        count = lax.axis_size(axis)
        ends = count - 1
        head = lax.slice_in_dim(cells, 0, width, axis=dim)
        tail = lax.slice_in_dim(cells, cells.shape[dim] - width, cells.shape[dim], axis=dim)
        cells = jnp.concatenate(
            [
                lax.ppermute(tail, axis, [(i, (i + 1) % count) for i in range(ends)]),
                cells,
                lax.ppermute(head, axis, [((i + 1) % count, i) for i in range(ends)]),
            ],
            axis=dim,
        )
    return cells


def gate_update(padded, cell_prev, kernel, offset):
    batch = padded.shape[0]
    height = padded.shape[1] - 2
    width = padded.shape[2] - 2
    chans = padded.shape[3]
    gates = jnp.zeros((batch * height * width, kernel.shape[-1]), jnp.float32)
    for tap in range(9):
        dy = tap // 3
        dx = tap % 3
        window = padded[:, dy : dy + height, dx : dx + width, :].reshape(-1, chans)
        gates = gates + jnp.dot(window, kernel[tap], preferred_element_type=jnp.float32)
    gates = (gates + offset[None, :]).reshape(batch, height, width, -1)
    quarter = gates.shape[-1] // 4
    gate_i = jax.nn.sigmoid(gates[..., :quarter])
    gate_f = jax.nn.sigmoid(gates[..., quarter : 2 * quarter])
    gate_g = jnp.tanh(gates[..., 2 * quarter : 3 * quarter])
    gate_o = jax.nn.sigmoid(gates[..., 3 * quarter :])
    cell = gate_f * cell_prev + gate_i * gate_g
    hidden = (gate_o * jnp.tanh(cell)).astype(jnp.bfloat16)
    return (hidden, cell)


def on_device(latent, hidden_old, cell_old, weights, bias):
    kernel = weights[0]
    offset = bias[0]
    hidden_prev = hidden_old[0]
    cell_prev = cell_old[0]
    section_idx = lax.axis_index("section")
    sections = lax.axis_size("section")
    count = 1
    hidden_acc = jnp.zeros_like(hidden_prev)
    cell_acc = jnp.zeros_like(cell_prev)
    outgoing = None
    for tick in range(count + sections - 1):
        micro = tick - section_idx
        if tick == 0:
            layer_in = latent
        else:
            received = shifted(outgoing, "section", 1)
            layer_in = jnp.where(section_idx == 0, latent, received)
        stacked = jnp.concatenate([layer_in, hidden_prev], axis=-1)
        padded = padded_2(stacked, (("row", 1), ("col", 2)), 1)
        hidden_step, cell_step = gate_update(padded, cell_prev, kernel, offset)
        active = (micro >= 0) & (micro < count)
        hidden_acc = jnp.where(active, hidden_step, hidden_acc)
        cell_acc = jnp.where(active, cell_step, cell_acc)
        outgoing = hidden_step
    return (hidden_acc[None], cell_acc[None])


def solution(mesh):
    in_specs = (
        P(None, "row", "col", None),
        P("section", None, "row", "col", None),
        P("section", None, "row", "col", None),
        P("section", None, None, None),
        P("section", None),
    )
    out_specs = (P("section", None, "row", "col", None), P("section", None, "row", "col", None))
    return jax.shard_map(
        on_device, mesh=mesh, in_specs=in_specs, out_specs=out_specs, check_vma=False
    )
```

profile of v0, /device:TPU:4, one launch (start us, length us, event | category | flops | bytes accessed | tf_op | source)
XLA Modules:
  0.0 97.8 jit_solution(13758964996315218813)
XLA Ops:
  1.5 1.7 %collective-permute-start = (bf16[2,1,16,256]{3,2,1,0:T(8,128)(2,1)S(1)}, bf16[2,1,16,256]{3,2,1,0:T(8,128)(2,1)S(1)}, u32[]{:S(2)}, u32[]{:S(2)}) collective-permute-start(bf16[2,1,16,256]{3,2,1,0:T(8,128)(2,1)S(1)} %get-tuple-element.10), channel_id=1, source_target_pairs={{0,4},{1,5},{2,6},{3,7},{8,12},{9,13},{10,14},{11,15},{16,20},{17,... | collective-permute-start | bytes 49160 | tf_op jit(solution)/shard_map/ppermute | solution.py:21
  3.2 1.3 %collective-permute-start.1 = (bf16[2,1,16,256]{3,2,1,0:T(8,128)(2,1)S(1)}, bf16[2,1,16,256]{3,2,1,0:T(8,128)(2,1)S(1)}, u32[]{:S(2)}, u32[]{:S(2)}) collective-permute-start(bf16[2,1,16,256]{3,2,1,0:T(8,128)(2,1)S(1)} %get-tuple-element.68), channel_id=1, source_target_pairs={{4,0},{5,1},{6,2},{7,3},{12,8},{13,9},{14,10},{15,11},{20,16},{21,... | collective-permute-start | bytes 49160 | tf_op jit(solution)/shard_map/ppermute | solution.py:23
  4.5 1.8 %collective-permute-done.1 = bf16[2,1,16,256]{3,2,1,0:T(8,128)(2,1)S(1)} collective-permute-done((bf16[2,1,16,256]{3,2,1,0:T(8,128)(2,1)S(1)}, bf16[2,1,16,256]{3,2,1,0:T(8,128)(2,1)S(1)}, u32[]{:S(2)}, u32[]{:S(2)}) %collective-permute-start.1) | collective-permute-done | bytes 16416 | tf_op jit(solution)/shard_map/ppermute | solution.py:23
  7.4 3.5 %collective-permute-start.2 = (bf16[2,18,1,256]{3,2,1,0:T(2,128)(2,1)S(1)}, bf16[2,18,1,256]{3,2,1,0:T(2,128)(2,1)S(1)}, u32[]{:S(2)}, u32[]{:S(2)}) collective-permute-start(bf16[2,18,1,256]{3,2,1,0:T(2,128)(2,1)S(1)} %get-tuple-element.52), channel_id=1, source_target_pairs={{0,1},{1,2},{2,3},{4,5},{5,6},{6,7},{8,9},{9,10},{10,11},{12,13},{... | collective-permute-start | bytes 55304 | tf_op jit(solution)/shard_map/ppermute | solution.py:21
  10.9 1.3 %collective-permute-start.3 = (bf16[2,18,1,256]{3,2,1,0:T(2,128)(2,1)S(1)}, bf16[2,18,1,256]{3,2,1,0:T(2,128)(2,1)S(1)}, u32[]{:S(2)}, u32[]{:S(2)}) collective-permute-start(bf16[2,18,1,256]{3,2,1,0:T(2,128)(2,1)S(1)} %get-tuple-element.53), channel_id=1, source_target_pairs={{1,0},{2,1},{3,2},{5,4},{6,5},{7,6},{9,8},{10,9},{11,10},{13,12},{... | collective-permute-start | bytes 55304 | tf_op jit(solution)/shard_map/ppermute | solution.py:23
  12.2 1.2 %fusion.44 = (bf16[2,16,16,256]{3,2,1,0:T(8,128)(2,1)S(1)}, bf16[2,16,16,256]{3,2,1,0:T(8,128)(2,1)S(1)}) fusion(bf16[2,16,16,128]{3,2,1,0:T(8,128)(2,1)} %bitcast.171, bf16[2,1,16,256]{3,2,1,0:T(8,128)(2,1)S(1)} %collective-permute-done.1, bf16[2,16,16,128]{3,2,1,0:T(8,128)(2,1)} %param.5, bf16[2,1,16,256]{3,2,1,0:T(8,128)(2,1)S(1)} %collective-permute-done), kind=kLoop, calls=%fused_computation.96 | loop fusion | flops 1572864 | bytes 819200 | tf_op jit(solution)/shard_map/concatenate | solution.py:19
  13.3 1.2 %fusion.142 = f32[512,512]{1,0:T(8,128)S(1)} fusion(bf16[512,256]{1,0:T(8,128)(2,1)S(1)} %bitcast.220, bf16[1,9,256,512]{3,2,1,0:T(8,128)(2,1)} %param.8), kind=kOutput, calls=%fused_computation.210 | convolution fusion | flops 134217728 | bytes 1572864 | tf_op jit(solution)/shard_map/dot_general | solution.py:40
  14.6 2.1 %collective-permute-done.3 = bf16[2,18,1,256]{3,2,1,0:T(2,128)(2,1)S(1)} collective-permute-done((bf16[2,18,1,256]{3,2,1,0:T(2,128)(2,1)S(1)}, bf16[2,18,1,256]{3,2,1,0:T(2,128)(2,1)S(1)}, u32[]{:S(2)}, u32[]{:S(2)}) %collective-permute-start.3) | collective-permute-done | bytes 18464 | tf_op jit(solution)/shard_map/ppermute | solution.py:23
  20.5 3.4 %collective-permute-start.4 = (bf16[2,16,16,128]{3,2,1,0:T(8,128)(2,1)S(1)}, bf16[2,16,16,128]{3,2,1,0:T(8,128)(2,1)S(1)}, u32[]{:S(2)}, u32[]{:S(2)}) collective-permute-start(bf16[2,16,16,128]{3,2,1,0:T(8,128)(2,1)S(1)} %get-tuple-element.8), channel_id=1, source_target_pairs={{0,8},{8,16},{16,24},{1,9},{9,17},{17,25},{2,10},{10,18},{18,26},{... | collective-permute-start | bytes 393224 | tf_op jit(solution)/shard_map/ppermute | solution.py:10
  23.9 4.4 %collective-permute-done.4 = bf16[2,16,16,128]{3,2,1,0:T(8,128)(2,1)S(1)} collective-permute-done((bf16[2,16,16,128]{3,2,1,0:T(8,128)(2,1)S(1)}, bf16[2,16,16,128]{3,2,1,0:T(8,128)(2,1)S(1)}, u32[]{:S(2)}, u32[]{:S(2)}) %collective-permute-start.4) | collective-permute-done | bytes 131104 | tf_op jit(solution)/shard_map/ppermute | solution.py:10
  28.3 1.3 %collective-permute-start.5 = (bf16[2,1,16,256]{3,2,1,0:T(8,128)(2,1)S(1)}, bf16[2,1,16,256]{3,2,1,0:T(8,128)(2,1)S(1)}, u32[]{:S(2)}, u32[]{:S(2)}) collective-permute-start(bf16[2,1,16,256]{3,2,1,0:T(8,128)(2,1)S(1)} %get-tuple-element.66), channel_id=1, source_target_pairs={{0,4},{1,5},{2,6},{3,7},{8,12},{9,13},{10,14},{11,15},{16,20},{17,... | collective-permute-start | bytes 49160 | tf_op jit(solution)/shard_map/ppermute | solution.py:21
  29.6 1.3 %collective-permute-start.6 = (bf16[2,1,16,256]{3,2,1,0:T(8,128)(2,1)S(1)}, bf16[2,1,16,256]{3,2,1,0:T(8,128)(2,1)S(1)}, u32[]{:S(2)}, u32[]{:S(2)}) collective-permute-start(bf16[2,1,16,256]{3,2,1,0:T(8,128)(2,1)S(1)} %get-tuple-element.67), channel_id=1, source_target_pairs={{4,0},{5,1},{6,2},{7,3},{12,8},{13,9},{14,10},{15,11},{20,16},{21,... | collective-permute-start | bytes 49160 | tf_op jit(solution)/shard_map/ppermute | solution.py:23
  30.9 1.8 %collective-permute-done.6 = bf16[2,1,16,256]{3,2,1,0:T(8,128)(2,1)S(1)} collective-permute-done((bf16[2,1,16,256]{3,2,1,0:T(8,128)(2,1)S(1)}, bf16[2,1,16,256]{3,2,1,0:T(8,128)(2,1)S(1)}, u32[]{:S(2)}, u32[]{:S(2)}) %collective-permute-start.6) | collective-permute-done | bytes 16416 | tf_op jit(solution)/shard_map/ppermute | solution.py:23
  32.8 3.7 %collective-permute-start.7 = (bf16[2,18,1,256]{3,2,1,0:T(2,128)(2,1)S(1)}, bf16[2,18,1,256]{3,2,1,0:T(2,128)(2,1)S(1)}, u32[]{:S(2)}, u32[]{:S(2)}) collective-permute-start(bf16[2,18,1,256]{3,2,1,0:T(2,128)(2,1)S(1)} %get-tuple-element.48), channel_id=1, source_target_pairs={{0,1},{1,2},{2,3},{4,5},{5,6},{6,7},{8,9},{9,10},{10,11},{12,13},{... | collective-permute-start | bytes 55304 | tf_op jit(solution)/shard_map/ppermute | solution.py:21
  36.5 1.3 %collective-permute-start.8 = (bf16[2,18,1,256]{3,2,1,0:T(2,128)(2,1)S(1)}, bf16[2,18,1,256]{3,2,1,0:T(2,128)(2,1)S(1)}, u32[]{:S(2)}, u32[]{:S(2)}) collective-permute-start(bf16[2,18,1,256]{3,2,1,0:T(2,128)(2,1)S(1)} %get-tuple-element.49), channel_id=1, source_target_pairs={{1,0},{2,1},{3,2},{5,4},{6,5},{7,6},{9,8},{10,9},{11,10},{13,12},{... | collective-permute-start | bytes 55304 | tf_op jit(solution)/shard_map/ppermute | solution.py:23
  38.1 4.2 %collective-permute-done.8 = bf16[2,18,1,256]{3,2,1,0:T(2,128)(2,1)S(1)} collective-permute-done((bf16[2,18,1,256]{3,2,1,0:T(2,128)(2,1)S(1)}, bf16[2,18,1,256]{3,2,1,0:T(2,128)(2,1)S(1)}, u32[]{:S(2)}, u32[]{:S(2)}) %collective-permute-start.8) | collective-permute-done | bytes 18464 | tf_op jit(solution)/shard_map/ppermute | solution.py:23
  45.5 2.5 %collective-permute-start.9 = (bf16[2,16,16,128]{3,2,1,0:T(8,128)(2,1)S(1)}, bf16[2,16,16,128]{3,2,1,0:T(8,128)(2,1)S(1)}, u32[]{:S(2)}, u32[]{:S(2)}) collective-permute-start(bf16[2,16,16,128]{3,2,1,0:T(8,128)(2,1)S(1)} %get-tuple-element.6), channel_id=1, source_target_pairs={{0,8},{8,16},{16,24},{1,9},{9,17},{17,25},{2,10},{10,18},{18,26},{... | collective-permute-start | bytes 393224 | tf_op jit(solution)/shard_map/ppermute | solution.py:10
  48.0 5.2 %collective-permute-done.9 = bf16[2,16,16,128]{3,2,1,0:T(8,128)(2,1)S(1)} collective-permute-done((bf16[2,16,16,128]{3,2,1,0:T(8,128)(2,1)S(1)}, bf16[2,16,16,128]{3,2,1,0:T(8,128)(2,1)S(1)}, u32[]{:S(2)}, u32[]{:S(2)}) %collective-permute-start.9) | collective-permute-done | bytes 131104 | tf_op jit(solution)/shard_map/ppermute | solution.py:10
  53.3 1.3 %collective-permute-start.10 = (bf16[2,1,16,256]{3,2,1,0:T(8,128)(2,1)S(1)}, bf16[2,1,16,256]{3,2,1,0:T(8,128)(2,1)S(1)}, u32[]{:S(2)}, u32[]{:S(2)}) collective-permute-start(bf16[2,1,16,256]{3,2,1,0:T(8,128)(2,1)S(1)} %get-tuple-element.64), channel_id=1, source_target_pairs={{0,4},{1,5},{2,6},{3,7},{8,12},{9,13},{10,14},{11,15},{16,20},{17,... | collective-permute-start | bytes 49160 | tf_op jit(solution)/shard_map/ppermute | solution.py:21
  54.6 1.3 %collective-permute-start.11 = (bf16[2,1,16,256]{3,2,1,0:T(8,128)(2,1)S(1)}, bf16[2,1,16,256]{3,2,1,0:T(8,128)(2,1)S(1)}, u32[]{:S(2)}, u32[]{:S(2)}) collective-permute-start(bf16[2,1,16,256]{3,2,1,0:T(8,128)(2,1)S(1)} %get-tuple-element.65), channel_id=1, source_target_pairs={{4,0},{5,1},{6,2},{7,3},{12,8},{13,9},{14,10},{15,11},{20,16},{21,... | collective-permute-start | bytes 49160 | tf_op jit(solution)/shard_map/ppermute | solution.py:23
  55.9 1.8 %collective-permute-done.11 = bf16[2,1,16,256]{3,2,1,0:T(8,128)(2,1)S(1)} collective-permute-done((bf16[2,1,16,256]{3,2,1,0:T(8,128)(2,1)S(1)}, bf16[2,1,16,256]{3,2,1,0:T(8,128)(2,1)S(1)}, u32[]{:S(2)}, u32[]{:S(2)}) %collective-permute-start.11) | collective-permute-done | bytes 16416 | tf_op jit(solution)/shard_map/ppermute | solution.py:23
  57.8 3.5 %collective-permute-start.12 = (bf16[2,18,1,256]{3,2,1,0:T(2,128)(2,1)S(1)}, bf16[2,18,1,256]{3,2,1,0:T(2,128)(2,1)S(1)}, u32[]{:S(2)}, u32[]{:S(2)}) collective-permute-start(bf16[2,18,1,256]{3,2,1,0:T(2,128)(2,1)S(1)} %get-tuple-element.44), channel_id=1, source_target_pairs={{0,1},{1,2},{2,3},{4,5},{5,6},{6,7},{8,9},{9,10},{10,11},{12,13},{... | collective-permute-start | bytes 55304 | tf_op jit(solution)/shard_map/ppermute | solution.py:21
  61.3 1.3 %collective-permute-start.13 = (bf16[2,18,1,256]{3,2,1,0:T(2,128)(2,1)S(1)}, bf16[2,18,1,256]{3,2,1,0:T(2,128)(2,1)S(1)}, u32[]{:S(2)}, u32[]{:S(2)}) collective-permute-start(bf16[2,18,1,256]{3,2,1,0:T(2,128)(2,1)S(1)} %get-tuple-element.45), channel_id=1, source_target_pairs={{1,0},{2,1},{3,2},{5,4},{6,5},{7,6},{9,8},{10,9},{11,10},{13,12},{... | collective-permute-start | bytes 55304 | tf_op jit(solution)/shard_map/ppermute | solution.py:23
  62.9 4.2 %collective-permute-done.13 = bf16[2,18,1,256]{3,2,1,0:T(2,128)(2,1)S(1)} collective-permute-done((bf16[2,18,1,256]{3,2,1,0:T(2,128)(2,1)S(1)}, bf16[2,18,1,256]{3,2,1,0:T(2,128)(2,1)S(1)}, u32[]{:S(2)}, u32[]{:S(2)}) %collective-permute-start.13) | collective-permute-done | bytes 18464 | tf_op jit(solution)/shard_map/ppermute | solution.py:23
  71.0 1.9 %collective-permute-start.14 = (bf16[2,16,16,128]{3,2,1,0:T(8,128)(2,1)S(1)}, bf16[2,16,16,128]{3,2,1,0:T(8,128)(2,1)S(1)}, u32[]{:S(2)}, u32[]{:S(2)}) collective-permute-start(bf16[2,16,16,128]{3,2,1,0:T(8,128)(2,1)S(1)} %get-tuple-element.4), channel_id=1, source_target_pairs={{0,8},{8,16},{16,24},{1,9},{9,17},{17,25},{2,10},{10,18},{18,26},{... | collective-permute-start | bytes 393224 | tf_op jit(solution)/shard_map/ppermute | solution.py:10
  73.0 5.8 %collective-permute-done.14 = bf16[2,16,16,128]{3,2,1,0:T(8,128)(2,1)S(1)} collective-permute-done((bf16[2,16,16,128]{3,2,1,0:T(8,128)(2,1)S(1)}, bf16[2,16,16,128]{3,2,1,0:T(8,128)(2,1)S(1)}, u32[]{:S(2)}, u32[]{:S(2)}) %collective-permute-start.14) | collective-permute-done | bytes 131104 | tf_op jit(solution)/shard_map/ppermute | solution.py:10
  78.8 1.3 %collective-permute-start.15 = (bf16[2,1,16,256]{3,2,1,0:T(8,128)(2,1)S(1)}, bf16[2,1,16,256]{3,2,1,0:T(8,128)(2,1)S(1)}, u32[]{:S(2)}, u32[]{:S(2)}) collective-permute-start(bf16[2,1,16,256]{3,2,1,0:T(8,128)(2,1)S(1)} %get-tuple-element.62), channel_id=1, source_target_pairs={{0,4},{1,5},{2,6},{3,7},{8,12},{9,13},{10,14},{11,15},{16,20},{17,... | collective-permute-start | bytes 49160 | tf_op jit(solution)/shard_map/ppermute | solution.py:21
  80.1 1.3 %collective-permute-start.16 = (bf16[2,1,16,256]{3,2,1,0:T(8,128)(2,1)S(1)}, bf16[2,1,16,256]{3,2,1,0:T(8,128)(2,1)S(1)}, u32[]{:S(2)}, u32[]{:S(2)}) collective-permute-start(bf16[2,1,16,256]{3,2,1,0:T(8,128)(2,1)S(1)} %get-tuple-element.63), channel_id=1, source_target_pairs={{4,0},{5,1},{6,2},{7,3},{12,8},{13,9},{14,10},{15,11},{20,16},{21,... | collective-permute-start | bytes 49160 | tf_op jit(solution)/shard_map/ppermute | solution.py:23
  81.4 1.7 %collective-permute-done.16 = bf16[2,1,16,256]{3,2,1,0:T(8,128)(2,1)S(1)} collective-permute-done((bf16[2,1,16,256]{3,2,1,0:T(8,128)(2,1)S(1)}, bf16[2,1,16,256]{3,2,1,0:T(8,128)(2,1)S(1)}, u32[]{:S(2)}, u32[]{:S(2)}) %collective-permute-start.16) | collective-permute-done | bytes 16416 | tf_op jit(solution)/shard_map/ppermute | solution.py:23
  83.3 3.5 %collective-permute-start.17 = (bf16[2,18,1,256]{3,2,1,0:T(2,128)(2,1)S(1)}, bf16[2,18,1,256]{3,2,1,0:T(2,128)(2,1)S(1)}, u32[]{:S(2)}, u32[]{:S(2)}) collective-permute-start(bf16[2,18,1,256]{3,2,1,0:T(2,128)(2,1)S(1)} %get-tuple-element.40), channel_id=1, source_target_pairs={{0,1},{1,2},{2,3},{4,5},{5,6},{6,7},{8,9},{9,10},{10,11},{12,13},{... | collective-permute-start | bytes 55304 | tf_op jit(solution)/shard_map/ppermute | solution.py:21
  86.8 1.3 %collective-permute-start.18 = (bf16[2,18,1,256]{3,2,1,0:T(2,128)(2,1)S(1)}, bf16[2,18,1,256]{3,2,1,0:T(2,128)(2,1)S(1)}, u32[]{:S(2)}, u32[]{:S(2)}) collective-permute-start(bf16[2,18,1,256]{3,2,1,0:T(2,128)(2,1)S(1)} %get-tuple-element.41), channel_id=1, source_target_pairs={{1,0},{2,1},{3,2},{5,4},{6,5},{7,6},{9,8},{10,9},{11,10},{13,12},{... | collective-permute-start | bytes 55304 | tf_op jit(solution)/shard_map/ppermute | solution.py:23
  88.4 4.2 %collective-permute-done.18 = bf16[2,18,1,256]{3,2,1,0:T(2,128)(2,1)S(1)} collective-permute-done((bf16[2,18,1,256]{3,2,1,0:T(2,128)(2,1)S(1)}, bf16[2,18,1,256]{3,2,1,0:T(2,128)(2,1)S(1)}, u32[]{:S(2)}, u32[]{:S(2)}) %collective-permute-start.18) | collective-permute-done | bytes 18464 | tf_op jit(solution)/shard_map/ppermute | solution.py:23
  (109 shorter events, 18.9 us)
Async XLA Ops:
  0.6 16.1 %copy-start = (bf16[1,2,16,16,128]{4,3,2,1,0:T(8,128)(2,1)S(1)}, bf16[1,2,16,16,128]{4,3,2,1,0:T(8,128)(2,1)}, u32[]{:S(2)}) copy-start(bf16[1,2,16,16,128]{4,3,2,1,0:T(8,128)(2,1)} %param.6) | copy-start | bytes 393220
  0.6 16.1 %copy-start.2 = (bf16[2,16,16,128]{3,2,1,0:T(8,128)(2,1)S(1)}, bf16[2,16,16,128]{3,2,1,0:T(8,128)(2,1)}, u32[]{:S(2)}) copy-start(bf16[2,16,16,128]{3,2,1,0:T(8,128)(2,1)} %param.5) | copy-start | bytes 393220
  1.5 26.8 %copy-start.11 = (bf16[2,1,16,256]{3,2,1,0:T(8,128)(2,1)}, bf16[2,1,16,256]{3,2,1,0:T(8,128)(2,1)S(1)}, u32[]{:S(2)}) copy-start(bf16[2,1,16,256]{3,2,1,0:T(8,128)(2,1)S(1)} %get-tuple-element.69) | copy-start | bytes 49156
  1.5 3.0 %collective-permute-start = (bf16[2,1,16,256]{3,2,1,0:T(8,128)(2,1)S(1)}, bf16[2,1,16,256]{3,2,1,0:T(8,128)(2,1)S(1)}, u32[]{:S(2)}, u32[]{:S(2)}) collective-permute-start(bf16[2,1,16,256]{3,2,1,0:T(8,128)(2,1)S(1)} %get-tuple-element.10), channel_id=1, source_target_pairs={{0,4},{1,5},{2,6},{3,7},{8,12},{9,13},{10,14},{11,15},{16,20},{17,... | collective-permute-start | bytes 49160 | tf_op jit(solution)/shard_map/ppermute | solution.py:21
  3.2 3.1 %collective-permute-start.1 = (bf16[2,1,16,256]{3,2,1,0:T(8,128)(2,1)S(1)}, bf16[2,1,16,256]{3,2,1,0:T(8,128)(2,1)S(1)}, u32[]{:S(2)}, u32[]{:S(2)}) collective-permute-start(bf16[2,1,16,256]{3,2,1,0:T(8,128)(2,1)S(1)} %get-tuple-element.68), channel_id=1, source_target_pairs={{4,0},{5,1},{6,2},{7,3},{12,8},{13,9},{14,10},{15,11},{20,16},{21,... | collective-permute-start | bytes 49160 | tf_op jit(solution)/shard_map/ppermute | solution.py:23
  7.4 7.2 %collective-permute-start.2 = (bf16[2,18,1,256]{3,2,1,0:T(2,128)(2,1)S(1)}, bf16[2,18,1,256]{3,2,1,0:T(2,128)(2,1)S(1)}, u32[]{:S(2)}, u32[]{:S(2)}) collective-permute-start(bf16[2,18,1,256]{3,2,1,0:T(2,128)(2,1)S(1)} %get-tuple-element.52), channel_id=1, source_target_pairs={{0,1},{1,2},{2,3},{4,5},{5,6},{6,7},{8,9},{9,10},{10,11},{12,13},{... | collective-permute-start | bytes 55304 | tf_op jit(solution)/shard_map/ppermute | solution.py:21
  10.9 5.9 %collective-permute-start.3 = (bf16[2,18,1,256]{3,2,1,0:T(2,128)(2,1)S(1)}, bf16[2,18,1,256]{3,2,1,0:T(2,128)(2,1)S(1)}, u32[]{:S(2)}, u32[]{:S(2)}) collective-permute-start(bf16[2,18,1,256]{3,2,1,0:T(2,128)(2,1)S(1)} %get-tuple-element.53), channel_id=1, source_target_pairs={{1,0},{2,1},{3,2},{5,4},{6,5},{7,6},{9,8},{10,9},{11,10},{13,12},{... | collective-permute-start | bytes 55304 | tf_op jit(solution)/shard_map/ppermute | solution.py:23
  14.6 2.6 %copy-start.1 = (bf16[1,9,256,512]{3,2,1,0:T(8,128)(2,1)S(1)}, bf16[1,9,256,512]{3,2,1,0:T(8,128)(2,1)}, u32[]{:S(2)}) copy-start(bf16[1,9,256,512]{3,2,1,0:T(8,128)(2,1)} %param.8) | copy-start | bytes 7077892
  19.3 1.0 copy-start.3
  20.5 22.1 %copy-start.5 = (bf16[2,16,16,128]{3,2,1,0:T(8,128)(2,1)}, bf16[2,16,16,128]{3,2,1,0:T(8,128)(2,1)S(1)}, u32[]{:S(2)}) copy-start(bf16[2,16,16,128]{3,2,1,0:T(8,128)(2,1)S(1)} %get-tuple-element.8) | copy-start | bytes 393220
  20.5 7.8 %collective-permute-start.4 = (bf16[2,16,16,128]{3,2,1,0:T(8,128)(2,1)S(1)}, bf16[2,16,16,128]{3,2,1,0:T(8,128)(2,1)S(1)}, u32[]{:S(2)}, u32[]{:S(2)}) collective-permute-start(bf16[2,16,16,128]{3,2,1,0:T(8,128)(2,1)S(1)} %get-tuple-element.8), channel_id=1, source_target_pairs={{0,8},{8,16},{16,24},{1,9},{9,17},{17,25},{2,10},{10,18},{18,26},{... | collective-permute-start | bytes 393224 | tf_op jit(solution)/shard_map/ppermute | solution.py:10
  28.3 2.6 %collective-permute-start.5 = (bf16[2,1,16,256]{3,2,1,0:T(8,128)(2,1)S(1)}, bf16[2,1,16,256]{3,2,1,0:T(8,128)(2,1)S(1)}, u32[]{:S(2)}, u32[]{:S(2)}) collective-permute-start(bf16[2,1,16,256]{3,2,1,0:T(8,128)(2,1)S(1)} %get-tuple-element.66), channel_id=1, source_target_pairs={{0,4},{1,5},{2,6},{3,7},{8,12},{9,13},{10,14},{11,15},{16,20},{17,... | collective-permute-start | bytes 49160 | tf_op jit(solution)/shard_map/ppermute | solution.py:21
  29.6 3.1 %collective-permute-start.6 = (bf16[2,1,16,256]{3,2,1,0:T(8,128)(2,1)S(1)}, bf16[2,1,16,256]{3,2,1,0:T(8,128)(2,1)S(1)}, u32[]{:S(2)}, u32[]{:S(2)}) collective-permute-start(bf16[2,1,16,256]{3,2,1,0:T(8,128)(2,1)S(1)} %get-tuple-element.67), channel_id=1, source_target_pairs={{4,0},{5,1},{6,2},{7,3},{12,8},{13,9},{14,10},{15,11},{20,16},{21,... | collective-permute-start | bytes 49160 | tf_op jit(solution)/shard_map/ppermute | solution.py:23
  32.8 5.3 %collective-permute-start.7 = (bf16[2,18,1,256]{3,2,1,0:T(2,128)(2,1)S(1)}, bf16[2,18,1,256]{3,2,1,0:T(2,128)(2,1)S(1)}, u32[]{:S(2)}, u32[]{:S(2)}) collective-permute-start(bf16[2,18,1,256]{3,2,1,0:T(2,128)(2,1)S(1)} %get-tuple-element.48), channel_id=1, source_target_pairs={{0,1},{1,2},{2,3},{4,5},{5,6},{6,7},{8,9},{9,10},{10,11},{12,13},{... | collective-permute-start | bytes 55304 | tf_op jit(solution)/shard_map/ppermute | solution.py:21
  36.5 5.9 %collective-permute-start.8 = (bf16[2,18,1,256]{3,2,1,0:T(2,128)(2,1)S(1)}, bf16[2,18,1,256]{3,2,1,0:T(2,128)(2,1)S(1)}, u32[]{:S(2)}, u32[]{:S(2)}) collective-permute-start(bf16[2,18,1,256]{3,2,1,0:T(2,128)(2,1)S(1)} %get-tuple-element.49), channel_id=1, source_target_pairs={{1,0},{2,1},{3,2},{5,4},{6,5},{7,6},{9,8},{10,9},{11,10},{13,12},{... | collective-permute-start | bytes 55304 | tf_op jit(solution)/shard_map/ppermute | solution.py:23
  44.9 8.4 %copy-start.12 = (bf16[2,1,16,256]{3,2,1,0:T(8,128)(2,1)S(1)}, bf16[2,1,16,256]{3,2,1,0:T(8,128)(2,1)}, u32[]{:S(2)}) copy-start(bf16[2,1,16,256]{3,2,1,0:T(8,128)(2,1)} %copy-done.11) | copy-start | bytes 49156
  45.5 21.9 %copy-start.7 = (bf16[2,16,16,128]{3,2,1,0:T(8,128)(2,1)}, bf16[2,16,16,128]{3,2,1,0:T(8,128)(2,1)S(1)}, u32[]{:S(2)}) copy-start(bf16[2,16,16,128]{3,2,1,0:T(8,128)(2,1)S(1)} %get-tuple-element.6) | copy-start | bytes 393220
  45.5 7.8 %collective-permute-start.9 = (bf16[2,16,16,128]{3,2,1,0:T(8,128)(2,1)S(1)}, bf16[2,16,16,128]{3,2,1,0:T(8,128)(2,1)S(1)}, u32[]{:S(2)}, u32[]{:S(2)}) collective-permute-start(bf16[2,16,16,128]{3,2,1,0:T(8,128)(2,1)S(1)} %get-tuple-element.6), channel_id=1, source_target_pairs={{0,8},{8,16},{16,24},{1,9},{9,17},{17,25},{2,10},{10,18},{18,26},{... | collective-permute-start | bytes 393224 | tf_op jit(solution)/shard_map/ppermute | solution.py:10
  53.3 2.6 %collective-permute-start.10 = (bf16[2,1,16,256]{3,2,1,0:T(8,128)(2,1)S(1)}, bf16[2,1,16,256]{3,2,1,0:T(8,128)(2,1)S(1)}, u32[]{:S(2)}, u32[]{:S(2)}) collective-permute-start(bf16[2,1,16,256]{3,2,1,0:T(8,128)(2,1)S(1)} %get-tuple-element.64), channel_id=1, source_target_pairs={{0,4},{1,5},{2,6},{3,7},{8,12},{9,13},{10,14},{11,15},{16,20},{17,... | collective-permute-start | bytes 49160 | tf_op jit(solution)/shard_map/ppermute | solution.py:21
  54.6 3.1 %collective-permute-start.11 = (bf16[2,1,16,256]{3,2,1,0:T(8,128)(2,1)S(1)}, bf16[2,1,16,256]{3,2,1,0:T(8,128)(2,1)S(1)}, u32[]{:S(2)}, u32[]{:S(2)}) collective-permute-start(bf16[2,1,16,256]{3,2,1,0:T(8,128)(2,1)S(1)} %get-tuple-element.65), channel_id=1, source_target_pairs={{4,0},{5,1},{6,2},{7,3},{12,8},{13,9},{14,10},{15,11},{20,16},{21,... | collective-permute-start | bytes 49160 | tf_op jit(solution)/shard_map/ppermute | solution.py:23
  57.8 5.1 %collective-permute-start.12 = (bf16[2,18,1,256]{3,2,1,0:T(2,128)(2,1)S(1)}, bf16[2,18,1,256]{3,2,1,0:T(2,128)(2,1)S(1)}, u32[]{:S(2)}, u32[]{:S(2)}) collective-permute-start(bf16[2,18,1,256]{3,2,1,0:T(2,128)(2,1)S(1)} %get-tuple-element.44), channel_id=1, source_target_pairs={{0,1},{1,2},{2,3},{4,5},{5,6},{6,7},{8,9},{9,10},{10,11},{12,13},{... | collective-permute-start | bytes 55304 | tf_op jit(solution)/shard_map/ppermute | solution.py:21
  61.3 5.9 %collective-permute-start.13 = (bf16[2,18,1,256]{3,2,1,0:T(2,128)(2,1)S(1)}, bf16[2,18,1,256]{3,2,1,0:T(2,128)(2,1)S(1)}, u32[]{:S(2)}, u32[]{:S(2)}) collective-permute-start(bf16[2,18,1,256]{3,2,1,0:T(2,128)(2,1)S(1)} %get-tuple-element.45), channel_id=1, source_target_pairs={{1,0},{2,1},{3,2},{5,4},{6,5},{7,6},{9,8},{10,9},{11,10},{13,12},{... | collective-permute-start | bytes 55304 | tf_op jit(solution)/shard_map/ppermute | solution.py:23
  71.0 1.9 %copy-start.9 = (bf16[2,16,16,128]{3,2,1,0:T(8,128)(2,1)}, bf16[2,16,16,128]{3,2,1,0:T(8,128)(2,1)S(1)}, u32[]{:S(2)}) copy-start(bf16[2,16,16,128]{3,2,1,0:T(8,128)(2,1)S(1)} %get-tuple-element.4) | copy-start | bytes 393220
  71.0 7.7 %collective-permute-start.14 = (bf16[2,16,16,128]{3,2,1,0:T(8,128)(2,1)S(1)}, bf16[2,16,16,128]{3,2,1,0:T(8,128)(2,1)S(1)}, u32[]{:S(2)}, u32[]{:S(2)}) collective-permute-start(bf16[2,16,16,128]{3,2,1,0:T(8,128)(2,1)S(1)} %get-tuple-element.4), channel_id=1, source_target_pairs={{0,8},{8,16},{16,24},{1,9},{9,17},{17,25},{2,10},{10,18},{18,26},{... | collective-permute-start | bytes 393224 | tf_op jit(solution)/shard_map/ppermute | solution.py:10
  78.8 2.6 %collective-permute-start.15 = (bf16[2,1,16,256]{3,2,1,0:T(8,128)(2,1)S(1)}, bf16[2,1,16,256]{3,2,1,0:T(8,128)(2,1)S(1)}, u32[]{:S(2)}, u32[]{:S(2)}) collective-permute-start(bf16[2,1,16,256]{3,2,1,0:T(8,128)(2,1)S(1)} %get-tuple-element.62), channel_id=1, source_target_pairs={{0,4},{1,5},{2,6},{3,7},{8,12},{9,13},{10,14},{11,15},{16,20},{17,... | collective-permute-start | bytes 49160 | tf_op jit(solution)/shard_map/ppermute | solution.py:21
  80.1 3.1 %collective-permute-start.16 = (bf16[2,1,16,256]{3,2,1,0:T(8,128)(2,1)S(1)}, bf16[2,1,16,256]{3,2,1,0:T(8,128)(2,1)S(1)}, u32[]{:S(2)}, u32[]{:S(2)}) collective-permute-start(bf16[2,1,16,256]{3,2,1,0:T(8,128)(2,1)S(1)} %get-tuple-element.63), channel_id=1, source_target_pairs={{4,0},{5,1},{6,2},{7,3},{12,8},{13,9},{14,10},{15,11},{20,16},{21,... | collective-permute-start | bytes 49160 | tf_op jit(solution)/shard_map/ppermute | solution.py:23
  83.3 5.1 %collective-permute-start.17 = (bf16[2,18,1,256]{3,2,1,0:T(2,128)(2,1)S(1)}, bf16[2,18,1,256]{3,2,1,0:T(2,128)(2,1)S(1)}, u32[]{:S(2)}, u32[]{:S(2)}) collective-permute-start(bf16[2,18,1,256]{3,2,1,0:T(2,128)(2,1)S(1)} %get-tuple-element.40), channel_id=1, source_target_pairs={{0,1},{1,2},{2,3},{4,5},{5,6},{6,7},{8,9},{9,10},{10,11},{12,13},{... | collective-permute-start | bytes 55304 | tf_op jit(solution)/shard_map/ppermute | solution.py:21
  86.8 5.9 %collective-permute-start.18 = (bf16[2,18,1,256]{3,2,1,0:T(2,128)(2,1)S(1)}, bf16[2,18,1,256]{3,2,1,0:T(2,128)(2,1)S(1)}, u32[]{:S(2)}, u32[]{:S(2)}) collective-permute-start(bf16[2,18,1,256]{3,2,1,0:T(2,128)(2,1)S(1)} %get-tuple-element.41), channel_id=1, source_target_pairs={{1,0},{2,1},{3,2},{5,4},{6,5},{7,6},{9,8},{10,9},{11,10},{13,12},{... | collective-permute-start | bytes 55304 | tf_op jit(solution)/shard_map/ppermute | solution.py:23
  95.2 1.0 copy-start.4
  95.2 1.8 %copy-start.6 = (bf16[2,16,16,128]{3,2,1,0:T(8,128)(2,1)S(1)}, bf16[2,16,16,128]{3,2,1,0:T(8,128)(2,1)}, u32[]{:S(2)}) copy-start(bf16[2,16,16,128]{3,2,1,0:T(8,128)(2,1)} %copy-done.5) | copy-start | bytes 393220
  95.2 1.8 %copy-start.8 = (bf16[2,16,16,128]{3,2,1,0:T(8,128)(2,1)S(1)}, bf16[2,16,16,128]{3,2,1,0:T(8,128)(2,1)}, u32[]{:S(2)}) copy-start(bf16[2,16,16,128]{3,2,1,0:T(8,128)(2,1)} %copy-done.7) | copy-start | bytes 393220
  95.2 1.8 %copy-start.10 = (bf16[2,16,16,128]{3,2,1,0:T(8,128)(2,1)S(1)}, bf16[2,16,16,128]{3,2,1,0:T(8,128)(2,1)}, u32[]{:S(2)}) copy-start(bf16[2,16,16,128]{3,2,1,0:T(8,128)(2,1)} %copy-done.9) | copy-start | bytes 393220
  (3 other events, 2.1 us)
where the time goes:
time: 98.6 us; the launch traced here: 97.8 us
  starting transfers between devices  37.9 us (38%)
  waiting for transfers between devices  37.2 us (38%)
  matrix products  11.5 us (12%)
  other arithmetic  7.56 us (8%)
  local copies, waits for them, and re-layouts  2.27 us (2%)
  between operations  1.4 us (1%)
    ppermute x8, waiting for transfers between devices, padded_2(): lax.ppermute(head, axis, [((i + 1) % count, i) for i in range(ends)])  21.8 us
    ppermute x8, starting transfers between devices, padded_2(): lax.ppermute(tail, axis, [(i, (i + 1) % count) for i in range(ends)])  19.7 us
    ppermute x3, waiting for transfers between devices, shifted(): return lax.ppermute(x, axis, pairs)  15.4 us
    dot_general x36, matrix products, gate_update(): jnp.dot(window, kernel[tap], preferred_element_type=jnp.float32)  11.5 us
    ppermute x8, starting transfers between devices, padded_2(): lax.ppermute(head, axis, [((i + 1) % count, i) for i in range(ends)])  10.3 us
    ppermute x3, starting transfers between devices, shifted(): return lax.ppermute(x, axis, pairs)  7.81 us
    concatenate x12, other arithmetic, padded_2(): jnp.concatenate([lax.ppermute(tail, axis, [(i, (i + 1) % count) for i in...  3.42 us
  transfers between devices with their start and end apart: 19, of which 11 were waited for; matrix products, arithmetic and copies ran while one was open for 3% of the time, Pallas kernels for 0%

commit v1 on v0

v1 whole, which is shorter than its diff:
```python
import functools

import jax
import jax.numpy as jnp
from jax import lax
from jax.experimental import pallas as pl
from jax.experimental.pallas import tpu as pltpu
from jax.sharding import PartitionSpec as P

MESH = pl.DeviceIdType.MESH
F32 = jnp.float32
BF16 = jnp.bfloat16
AROUND = tuple((dr, dc) for dr in (-1, 0, 1) for dc in (-1, 0, 1) if (dr, dc) != (0, 0))
PAD = 8


def opposite(d):
    return len(AROUND) - 1 - d


def sigmoid(x):
    return 0.5 * jnp.tanh(0.5 * x) + 0.5


def kernel(
    sizes,
    latent_hbm,
    hidden_hbm,
    cell_hbm,
    weights_hbm,
    bias_ref,
    hidden_out,
    cell_out,
    latent,
    hidden,
    cell,
    w_in,
    w_own,
    main_in,
    halo_in,
    halo_own,
    own_edges,
    lat_edges,
    new_edges,
    new_hidden,
    new_cell,
    wide,
    taps,
    gates,
    load_sem,
    store_sem,
    own_send,
    own_recv,
    lat_send,
    in_recv,
    edge_send,
    main_send,
    main_recv,
):
    sections, rows, cols = sizes
    batch, height, width, chans = latent.shape
    half = height // 2
    s = lax.axis_index("section")
    r = lax.axis_index("row")
    c = lax.axis_index("col")
    first = s == 0
    feeds = s + 1 < sections

    def inside(dr, dc):
        return (r + dr >= 0) & (r + dr < rows) & (c + dc >= 0) & (c + dc < cols)

    def at(ds, dr, dc):
        return (s + ds, r + dr, c + dc)

    loads = [
        pltpu.make_async_copy(src, dst, load_sem.at[k])
        for k, (src, dst) in enumerate(
            (
                (hidden_hbm.at[0], hidden),
                (latent_hbm, latent),
                (weights_hbm.at[0, :, pl.ds(chans, chans)], w_own),
                (weights_hbm.at[0, :, pl.ds(0, chans)], w_in),
                (cell_hbm.at[0], cell),
            )
        )
    ]
    for load in loads:
        load.start()

    halo_in[...] = jnp.zeros_like(halo_in)
    halo_own[...] = jnp.zeros_like(halo_own)

    barrier = pltpu.get_barrier_semaphore()
    expected = jnp.int32(0)
    for dr, dc in AROUND + ((0, 0),):
        there = inside(dr, dc)
        if (dr, dc) != (0, 0):

            @pl.when(there)
            def _():
                pl.semaphore_signal(barrier, inc=1, device_id=at(0, dr, dc), device_id_type=MESH)

            expected = expected + there.astype(jnp.int32)

        @pl.when(there & (s > 0))
        def _():
            pl.semaphore_signal(barrier, inc=1, device_id=at(-1, dr, dc), device_id_type=MESH)

        expected = expected + (there & feeds).astype(jnp.int32)

    def pack(source, edges, b):
        tile = source[b].astype(F32)
        edges[0, b] = tile[:, 0, :].astype(BF16)
        edges[1, b] = tile[:, width - 1, :].astype(BF16)

    loads[0].wait()
    for b in range(batch):
        pack(hidden, own_edges, b)
    loads[1].wait()

    @pl.when(first)
    def _():
        for b in range(batch):
            pack(latent, lat_edges, b)

    pl.semaphore_wait(barrier, expected)

    def edge(tile, edges, b, dr, dc):
        if dr == 0:
            return edges.at[0 if dc < 0 else 1, b]
        return tile.at[b, 0 if dr < 0 else height - 1]

    def own_copy(d, b):
        dr, dc = AROUND[d]
        back = opposite(d)
        return pltpu.make_async_remote_copy(
            src_ref=edge(hidden, own_edges, b, dr, dc),
            dst_ref=halo_own.at[back, b],
            send_sem=own_send.at[d, b],
            recv_sem=own_recv.at[back, b],
            device_id=at(0, dr, dc),
            device_id_type=MESH,
        )

    def lat_copy(d, b):
        dr, dc = AROUND[d]
        back = opposite(d)
        return pltpu.make_async_remote_copy(
            src_ref=edge(latent, lat_edges, b, dr, dc),
            dst_ref=halo_in.at[back, b],
            send_sem=lat_send.at[d, b],
            recv_sem=in_recv.at[back, b],
            device_id=at(0, dr, dc),
            device_id_type=MESH,
        )

    def edge_copy(d, b):
        dr, dc = AROUND[d]
        back = opposite(d)
        return pltpu.make_async_remote_copy(
            src_ref=edge(new_hidden, new_edges, b, dr, dc),
            dst_ref=halo_in.at[back, b],
            send_sem=edge_send.at[d, b],
            recv_sem=in_recv.at[back, b],
            device_id=at(1, dr, dc),
            device_id_type=MESH,
        )

    def main_copy(b, part):
        span = pl.ds(part * half, half)
        return pltpu.make_async_remote_copy(
            src_ref=new_hidden.at[b, span],
            dst_ref=main_in.at[b, span],
            send_sem=main_send.at[b, part],
            recv_sem=main_recv.at[b, part],
            device_id=at(1, 0, 0),
            device_id_type=MESH,
        )

    for b in range(batch):
        for d, (dr, dc) in enumerate(AROUND):

            @pl.when(inside(dr, dc))
            def _():
                own_copy(d, b).start()

            @pl.when(inside(dr, dc) & first)
            def _():
                lat_copy(d, b).start()

    def convolved(main, halo, w):
        left, right = PAD - 1, PAD + width
        wide[1 : height + 1, PAD : PAD + width, :] = main.astype(F32)
        for d, (dr, dc) in enumerate(AROUND):
            strip = halo(d).astype(F32)
            line = 0 if dr < 0 else height + 1
            if dr == 0:
                side = left if dc < 0 else right
                wide[1 : height + 1, side : side + 1, :] = strip.reshape(height, 1, chans)
            elif dc == 0:
                wide[line, PAD : PAD + width, :] = strip
            elif dc < 0:
                wide[line, left : left + 1, :] = strip[width - 1 : width]
            else:
                wide[line, right : right + 1, :] = strip[0:1]
        for dx in range(3):
            taps[:, :, dx * chans : (dx + 1) * chans] = wide[
                :, left + dx : left + dx + width, :
            ].astype(BF16)
        patch = jnp.concatenate(
            [
                taps[dy : dy + height].reshape(height * width, 3 * chans)
                for dy in range(3)
            ],
            axis=-1,
        )
        return jnp.dot(patch, w[...].reshape(9 * chans, -1), preferred_element_type=F32)

    stores = []
    for b in range(batch):
        for d, (dr, dc) in enumerate(AROUND):

            @pl.when(inside(dr, dc))
            def _():
                own_copy(opposite(d), b).wait_recv()

        if b == 0:
            loads[2].wait()
        gates[...] = convolved(hidden[b], lambda d: halo_own[d, b], w_own) + bias_ref[...]

        @pl.when(first)
        def _():
            main_in[b] = latent[b]

        for d, (dr, dc) in enumerate(AROUND):

            @pl.when(inside(dr, dc))
            def _():
                edge_copy(opposite(d), b).wait_recv()

        for part in range(2):

            @pl.when(s > 0)
            def _():
                main_copy(b, part).wait_recv()

        if b == 0:
            loads[3].wait()
        gates[...] += convolved(main_in[b], lambda d: halo_in[d, b], w_in)
        if b == 0:
            loads[4].wait()
        for part in range(2):
            span = pl.ds(part * half, half)
            z = gates[part * half * width : (part + 1) * half * width]
            old = cell[b, span].reshape(half * width, chans)
            gate_i = sigmoid(z[:, :chans])
            gate_f = sigmoid(z[:, chans : 2 * chans])
            gate_g = jnp.tanh(z[:, 2 * chans : 3 * chans])
            gate_o = sigmoid(z[:, 3 * chans :])
            now = gate_f * old + gate_i * gate_g
            new_cell[b, span] = now.reshape(half, width, chans)
            out = (gate_o * jnp.tanh(now)).astype(BF16).reshape(half, width, chans)
            new_hidden[b, span] = out
            tile = out.astype(F32)
            new_edges[0, b, span] = tile[:, 0, :].astype(BF16)
            new_edges[1, b, span] = tile[:, width - 1, :].astype(BF16)
            for d, (dr, dc) in enumerate(AROUND):
                if (part == 0) == (dr < 0):

                    @pl.when(inside(dr, dc) & feeds)
                    def _():
                        edge_copy(d, b).start()

            @pl.when(feeds)
            def _():
                main_copy(b, part).start()

        for k, (src, dst) in enumerate(((new_cell, cell_out), (new_hidden, hidden_out))):
            store = pltpu.make_async_copy(src.at[b], dst.at[0, b], store_sem.at[k, b])
            store.start()
            stores.append(store)

    for b in range(batch):
        for d, (dr, dc) in enumerate(AROUND):

            @pl.when(inside(dr, dc))
            def _():
                own_copy(d, b).wait_send()

            @pl.when(inside(dr, dc) & first)
            def _():
                lat_copy(d, b).wait_send()

            @pl.when(inside(dr, dc) & feeds)
            def _():
                edge_copy(d, b).wait_send()

        for part in range(2):

            @pl.when(feeds)
            def _():
                main_copy(b, part).wait_send()

    for store in stores:
        store.wait()


def on_device(latent, hidden_old, cell_old, weights, bias):
    sizes = tuple(lax.axis_size(axis) for axis in ("section", "row", "col"))
    batch, height, width, chans = latent.shape
    gate_chans = weights.shape[-1]
    around = len(AROUND)
    edge = max(height, width)
    assert height == width and height % 16 == 0
    tile = (batch, height, width, chans)
    dma = pltpu.SemaphoreType.DMA
    anywhere = pl.BlockSpec(memory_space=pl.ANY)
    flops = 2 * batch * height * width * 9 * 2 * chans * gate_chans
    return pl.pallas_call(
        functools.partial(kernel, sizes),
        out_shape=(
            jax.ShapeDtypeStruct(hidden_old.shape, BF16),
            jax.ShapeDtypeStruct(cell_old.shape, F32),
        ),
        in_specs=[anywhere] * 4 + [pl.BlockSpec(memory_space=pltpu.VMEM)],
        out_specs=(anywhere, anywhere),
        scratch_shapes=[
            pltpu.VMEM(tile, BF16),
            pltpu.VMEM(tile, BF16),
            pltpu.VMEM(tile, F32),
            pltpu.VMEM((9, chans, gate_chans), BF16),
            pltpu.VMEM((9, chans, gate_chans), BF16),
            pltpu.VMEM(tile, BF16),
            pltpu.VMEM((around, batch, edge, chans), BF16),
            pltpu.VMEM((around, batch, edge, chans), BF16),
            pltpu.VMEM((2, batch, edge, chans), BF16),
            pltpu.VMEM((2, batch, edge, chans), BF16),
            pltpu.VMEM((2, batch, edge, chans), BF16),
            pltpu.VMEM(tile, BF16),
            pltpu.VMEM(tile, F32),
            pltpu.VMEM((height + 2, width + 2 * PAD, chans), F32),
            pltpu.VMEM((height + 2, width, 3 * chans), BF16),
            pltpu.VMEM((height * width, gate_chans), F32),
            dma((5,)),
            dma((2, batch)),
            dma((around, batch)),
            dma((around, batch)),
            dma((around, batch)),
            dma((around, batch)),
            dma((around, batch)),
            dma((batch, 2)),
            dma((batch, 2)),
        ],
        compiler_params=pltpu.CompilerParams(
            collective_id=0, has_side_effects=True, vmem_limit_bytes=32 * 1024 * 1024
        ),
        cost_estimate=pl.CostEstimate(
            flops=flops, bytes_accessed=weights.size * 2, transcendentals=0
        ),
    )(latent, hidden_old, cell_old, weights, bias)


def solution(mesh):
    in_specs = (
        P(None, "row", "col", None),
        P("section", None, "row", "col", None),
        P("section", None, "row", "col", None),
        P("section", None, None, None),
        P("section", None),
    )
    out_specs = (P("section", None, "row", "col", None), P("section", None, "row", "col", None))
    return jax.shard_map(
        on_device, mesh=mesh, in_specs=in_specs, out_specs=out_specs, check_vma=False
    )
```

time: 98.6 us -> 31.7 us (0.32)
  the two profiles are of different devices: /device:TPU:4 before, /device:TPU:7 now
where the time goes in v1:
time: 31.7 us; the launch traced here: 31.1 us
  Pallas kernels  23.9 us (75%)
  local copies, waits for them, and re-layouts  6.46 us (20%)
  between operations  0.65 us (2%)
    pallas_call x1, Pallas kernels, on_device(): pl.pallas_call(functools.partial(kernel, sizes), out_shape=(jax.ShapeDtyp...  23.9 us
    unnamed x12, local copies, waits for them, and re-layouts  6.46 us

profile of v1, /device:TPU:7, one launch (start us, length us, event | category | flops | bytes accessed | tf_op | source)
XLA Modules:
  0.0 31.1 jit_solution(5212723947746167513)
XLA Ops:
  0.6 0.0 copy-start
  0.6 1.7 %copy-done = bf16[1,9,256,512]{3,2,1,0:T(8,128)(2,1)S(1)} copy-done((bf16[1,9,256,512]{3,2,1,0:T(8,128)(2,1)S(1)}, bf16[1,9,256,512]{3,2,1,0:T(8,128)(2,1)}, u32[]{:S(2)}) %copy-start) | copy-done | bytes 2359320
  2.3 0.0 copy-start.1
  2.3 0.9 %copy-done.1 = f32[1,2,16,16,128]{4,3,2,1,0:T(8,128)S(1)} copy-done((f32[1,2,16,16,128]{4,3,2,1,0:T(8,128)S(1)}, f32[1,2,16,16,128]{4,3,2,1,0:T(8,128)}, u32[]{:S(2)}) %copy-start.1) | copy-done | bytes 262168
  3.2 0.0 copy-start.2
  3.2 0.9 %copy-done.2 = bf16[2,16,16,128]{3,2,1,0:T(8,128)(2,1)S(1)} copy-done((bf16[2,16,16,128]{3,2,1,0:T(8,128)(2,1)S(1)}, bf16[2,16,16,128]{3,2,1,0:T(8,128)(2,1)}, u32[]{:S(2)}) %copy-start.2) | copy-done | bytes 131096
  4.2 0.0 copy-start.3
  4.2 0.9 %copy-done.3 = bf16[1,2,16,16,128]{4,3,2,1,0:T(8,128)(2,1)S(1)} copy-done((bf16[1,2,16,16,128]{4,3,2,1,0:T(8,128)(2,1)S(1)}, bf16[1,2,16,16,128]{4,3,2,1,0:T(8,128)(2,1)}, u32[]{:S(2)}) %copy-start.3) | copy-done | bytes 131096
  5.1 0.0 copy-start.4
  5.1 0.7 %copy-done.4 = f32[1,512]{1,0:T(1,128)S(1)} copy-done((f32[1,512]{1,0:T(1,128)S(1)}, f32[1,512]{1,0:T(1,128)}, u32[]{:S(2)}) %copy-start.4) | copy-done | bytes 2072
  5.7 23.9 %shard_map.68 = (bf16[1,2,16,16,128]{4,3,2,1,0:T(8,128)(2,1)S(1)}, f32[1,2,16,16,128]{4,3,2,1,0:T(8,128)S(1)}) custom-call(bf16[2,16,16,128]{3,2,1,0:T(8,128)(2,1)S(1)} %copy-done.2, bf16[1,2,16,16,128]{4,3,2,1,0:T(8,128)(2,1)S(1)} %copy-done.3, f32[1,2,16,16,128]{4,3,2,1,0:T(8,128)S(1)} %copy-done.1, bf16[1,9,256,512]{3,2,1,0:T(8,128)(2,1)S(1)} %copy-done, ...), custom_call_target="tpu_custom_call" | custom-call | flops 1207959552 | bytes 2359296 | tf_op jit(solution)/shard_map/pallas_call | solution.py:319
  29.7 0.7 %copy.9 = bf16[1,2,16,16,128]{4,3,2,1,0:T(8,128)(2,1)} copy(bf16[1,2,16,16,128]{4,3,2,1,0:T(8,128)(2,1)S(1)} %get-tuple-element.4) | data formatting | bytes 262144
  30.3 0.7 %copy.10 = f32[1,2,16,16,128]{4,3,2,1,0:T(8,128)} copy(f32[1,2,16,16,128]{4,3,2,1,0:T(8,128)S(1)} %get-tuple-element.5) | data formatting | bytes 524288
Async XLA Ops:
  0.6 1.7 %copy-start = (bf16[1,9,256,512]{3,2,1,0:T(8,128)(2,1)S(1)}, bf16[1,9,256,512]{3,2,1,0:T(8,128)(2,1)}, u32[]{:S(2)}) copy-start(bf16[1,9,256,512]{3,2,1,0:T(8,128)(2,1)} %weights_hbm.1) | copy-start | bytes 7077892
  2.3 0.9 %copy-start.1 = (f32[1,2,16,16,128]{4,3,2,1,0:T(8,128)S(1)}, f32[1,2,16,16,128]{4,3,2,1,0:T(8,128)}, u32[]{:S(2)}) copy-start(f32[1,2,16,16,128]{4,3,2,1,0:T(8,128)} %cell_hbm.1) | copy-start | bytes 786436
  3.2 0.9 %copy-start.2 = (bf16[2,16,16,128]{3,2,1,0:T(8,128)(2,1)S(1)}, bf16[2,16,16,128]{3,2,1,0:T(8,128)(2,1)}, u32[]{:S(2)}) copy-start(bf16[2,16,16,128]{3,2,1,0:T(8,128)(2,1)} %latent_hbm.1) | copy-start | bytes 393220
  4.2 0.9 %copy-start.3 = (bf16[1,2,16,16,128]{4,3,2,1,0:T(8,128)(2,1)S(1)}, bf16[1,2,16,16,128]{4,3,2,1,0:T(8,128)(2,1)}, u32[]{:S(2)}) copy-start(bf16[1,2,16,16,128]{4,3,2,1,0:T(8,128)(2,1)} %hidden_hbm.1) | copy-start | bytes 393220
  5.1 0.7 %copy-start.4 = (f32[1,512]{1,0:T(1,128)S(1)}, f32[1,512]{1,0:T(1,128)}, u32[]{:S(2)}) copy-start(f32[1,512]{1,0:T(1,128)} %bias_ref.1) | copy-start | bytes 6148

commit v2 on v1

--- a/solution.py
+++ b/solution.py
@@ -56,6 +56,7 @@
     edge_send,
     main_send,
     main_recv,
+    ready,
 ):
     sections, rows, cols = sizes
     batch, height, width, chans = latent.shape
@@ -92,6 +93,7 @@
 
     barrier = pltpu.get_barrier_semaphore()
     expected = jnp.int32(0)
+    listeners = jnp.int32(0)
     for dr, dc in AROUND + ((0, 0),):
         there = inside(dr, dc)
         if (dr, dc) != (0, 0):
@@ -102,11 +104,15 @@
 
             expected = expected + there.astype(jnp.int32)
 
-        @pl.when(there & (s > 0))
+    for dr, dc in AROUND + ((0, 0),):
+        there = inside(dr, dc)
+
+        @pl.when(there & feeds)
         def _():
-            pl.semaphore_signal(barrier, inc=1, device_id=at(-1, dr, dc), device_id_type=MESH)
-
-        expected = expected + (there & feeds).astype(jnp.int32)
+            pl.semaphore_signal(barrier, inc=1, device_id=at(1, dr, dc), device_id_type=MESH)
+
+        expected = expected + (there & (s > 0)).astype(jnp.int32)
+        listeners = listeners + (there & feeds).astype(jnp.int32)
 
     def pack(source, edges, b):
         tile = source[b].astype(F32)
@@ -124,6 +130,12 @@
             pack(latent, lat_edges, b)
 
     pl.semaphore_wait(barrier, expected)
+
+    for dr, dc in AROUND + ((0, 0),):
+
+        @pl.when(inside(dr, dc) & (s > 0))
+        def _():
+            pl.semaphore_signal(ready, inc=1, device_id=at(-1, dr, dc), device_id_type=MESH)
 
     def edge(tile, edges, b, dr, dc):
         if dr == 0:
@@ -249,6 +261,11 @@
         gates[...] += convolved(main_in[b], lambda d: halo_in[d, b], w_in)
         if b == 0:
             loads[4].wait()
+
+            @pl.when(feeds)
+            def _():
+                pl.semaphore_wait(ready, listeners)
+
         for part in range(2):
             span = pl.ds(part * half, half)
             z = gates[part * half * width : (part + 1) * half * width]
@@ -314,7 +331,7 @@
     assert height == width and height % 16 == 0
     tile = (batch, height, width, chans)
     dma = pltpu.SemaphoreType.DMA
-    anywhere = pl.BlockSpec(memory_space=pl.ANY)
+    anywhere = pl.BlockSpec(memory_space=pltpu.HBM)
     flops = 2 * batch * height * width * 9 * 2 * chans * gate_chans
     return pl.pallas_call(
         functools.partial(kernel, sizes),
@@ -350,9 +367,10 @@
             dma((around, batch)),
             dma((batch, 2)),
             dma((batch, 2)),
+            pltpu.SemaphoreType.REGULAR,
         ],
         compiler_params=pltpu.CompilerParams(
-            collective_id=0, has_side_effects=True, vmem_limit_bytes=32 * 1024 * 1024
+            collective_id=0, has_side_effects=True, vmem_limit_bytes=64 * 1024 * 1024 - 4096
         ),
         cost_estimate=pl.CostEstimate(
             flops=flops, bytes_accessed=weights.size * 2, transcendentals=0

time: 31.7 us -> 27.7 us (0.87)
  local copies, waits for them, and re-layouts: 6.46 us -> 3.24 us
  Pallas kernels: 23.9 us -> 23.4 us
    unnamed x12 -> x2, local copies, waits for them, and re-layouts: 6.46 us -> 3.24 us
    pallas_call x1, Pallas kernels: 23.9 us -> 23.4 us  [on_device(): pl.pallas_call(functools.partial(kernel, sizes), out_shape=(jax.ShapeDtyp...]
where the time goes in v2:
time: 27.7 us; the launch traced here: 27.3 us
  Pallas kernels  23.4 us (84%)
  local copies, waits for them, and re-layouts  3.24 us (12%)
  between operations  0.64 us (2%)
    pallas_call x1, Pallas kernels, on_device(): pl.pallas_call(functools.partial(kernel, sizes), out_shape=(jax.ShapeDtyp...  23.4 us
    unnamed x2, local copies, waits for them, and re-layouts  3.24 us

profile of v2, /device:TPU:7, one launch (start us, length us, event | category | flops | bytes accessed | tf_op | source)
XLA Modules:
  0.0 27.3 jit_solution(12262942199766775880)
XLA Ops:
  0.6 23.4 %shard_map.68 = (bf16[1,2,16,16,128]{4,3,2,1,0:T(8,128)(2,1)}, f32[1,2,16,16,128]{4,3,2,1,0:T(8,128)}) custom-call(bf16[2,16,16,128]{3,2,1,0:T(8,128)(2,1)} %latent_hbm.1, bf16[1,2,16,16,128]{4,3,2,1,0:T(8,128)(2,1)} %hidden_hbm.1, f32[1,2,16,16,128]{4,3,2,1,0:T(8,128)} %cell_hbm.1, bf16[1,9,256,512]{3,2,1,0:T(8,128)(2,1)} %weights_hbm.1, f32[1,512]{1,0:T(1,128)} %bias_ref.1), custom_call_target="tpu_custom_call" | custom-call | flops 1207959552 | bytes 2359296 | tf_op jit(solution)/shard_map/pallas_call | solution.py:336
  24.0 1.6 %copy.9 = bf16[1,2,16,16,128]{4,3,2,1,0:T(8,128)(2,1)} copy(bf16[1,2,16,16,128]{4,3,2,1,0:T(8,128)(2,1)} %get-tuple-element.4) | data formatting | bytes 262144
  25.6 1.7 %copy.10 = f32[1,2,16,16,128]{4,3,2,1,0:T(8,128)} copy(f32[1,2,16,16,128]{4,3,2,1,0:T(8,128)} %get-tuple-element.5) | data formatting | bytes 524288

commit v3 on v2

--- a/solution.py
+++ b/solution.py
@@ -15,7 +15,8 @@
 
 
 def opposite(d):
-    return len(AROUND) - 1 - d
+    dr, dc = AROUND[d]
+    return AROUND.index((dr, -dc))
 
 
 def sigmoid(x):
@@ -39,10 +40,12 @@
     main_in,
     halo_in,
     halo_own,
+    halo_lat,
     own_edges,
     lat_edges,
     new_edges,
     new_hidden,
+    out_hidden,
     new_cell,
     wide,
     taps,
@@ -52,6 +55,7 @@
     own_send,
     own_recv,
     lat_send,
+    lat_recv,
     in_recv,
     edge_send,
     main_send,
@@ -61,28 +65,37 @@
     sections, rows, cols = sizes
     batch, height, width, chans = latent.shape
     half = height // 2
+    least = half - (sections - 1)
     s = lax.axis_index("section")
     r = lax.axis_index("row")
     c = lax.axis_index("col")
     first = s == 0
     feeds = s + 1 < sections
+    odd = lax.rem(r, 2)
+    step = 1 - 2 * odd
+
+    def line(y):
+        return y + odd * (height - 1 - 2 * y)
+
+    def ordered(source, b, y0, y1):
+        return jnp.stack([source[b, line(y)] for y in range(y0, y1)])
 
     def inside(dr, dc):
-        return (r + dr >= 0) & (r + dr < rows) & (c + dc >= 0) & (c + dc < cols)
+        return (r + dr * step >= 0) & (r + dr * step < rows) & (c + dc >= 0) & (c + dc < cols)
 
     def at(ds, dr, dc):
-        return (s + ds, r + dr, c + dc)
+        return (s + ds, r + dr * step, c + dc)
+
+    def taps_of(dy, start):
+        return weights_hbm.at[0, pl.ds(3 * (dy + odd * (2 - 2 * dy)), 3), pl.ds(start, chans)]
 
     loads = [
         pltpu.make_async_copy(src, dst, load_sem.at[k])
         for k, (src, dst) in enumerate(
-            (
-                (hidden_hbm.at[0], hidden),
-                (latent_hbm, latent),
-                (weights_hbm.at[0, :, pl.ds(chans, chans)], w_own),
-                (weights_hbm.at[0, :, pl.ds(0, chans)], w_in),
-                (cell_hbm.at[0], cell),
-            )
+            [(hidden_hbm.at[0], hidden), (latent_hbm, latent)]
+            + [(taps_of(dy, chans), w_own.at[pl.ds(3 * dy, 3)]) for dy in range(3)]
+            + [(taps_of(dy, 0), w_in.at[pl.ds(3 * dy, 3)]) for dy in range(3)]
+            + [(cell_hbm.at[0], cell)]
         )
     ]
     for load in loads:
@@ -90,6 +103,7 @@
 
     halo_in[...] = jnp.zeros_like(halo_in)
     halo_own[...] = jnp.zeros_like(halo_own)
+    halo_lat[...] = jnp.zeros_like(halo_lat)
 
     barrier = pltpu.get_barrier_semaphore()
     expected = jnp.int32(0)
@@ -115,7 +129,7 @@
         listeners = listeners + (there & feeds).astype(jnp.int32)
 
     def pack(source, edges, b):
-        tile = source[b].astype(F32)
+        tile = ordered(source, b, 0, height).astype(F32)
         edges[0, b] = tile[:, 0, :].astype(BF16)
         edges[1, b] = tile[:, width - 1, :].astype(BF16)
 
@@ -140,7 +154,7 @@
     def edge(tile, edges, b, dr, dc):
         if dr == 0:
             return edges.at[0 if dc < 0 else 1, b]
-        return tile.at[b, 0 if dr < 0 else height - 1]
+        return tile.at[b, line(0 if dr < 0 else height - 1)]
 
     def own_copy(d, b):
         dr, dc = AROUND[d]
@@ -159,27 +173,36 @@
         back = opposite(d)
         return pltpu.make_async_remote_copy(
             src_ref=edge(latent, lat_edges, b, dr, dc),
-            dst_ref=halo_in.at[back, b],
+            dst_ref=halo_lat.at[back, b],
             send_sem=lat_send.at[d, b],
-            recv_sem=in_recv.at[back, b],
+            recv_sem=lat_recv.at[back, b],
             device_id=at(0, dr, dc),
             device_id_type=MESH,
         )
 
-    def edge_copy(d, b):
+    def edge_copy(d, b, part):
         dr, dc = AROUND[d]
         back = opposite(d)
+        if dr == 0:
+            src = new_edges.at[0 if dc < 0 else 1, b, part]
+        else:
+            src = new_hidden.at[b, 0 if dr < 0 else height - 1]
         return pltpu.make_async_remote_copy(
-            src_ref=edge(new_hidden, new_edges, b, dr, dc),
-            dst_ref=halo_in.at[back, b],
-            send_sem=edge_send.at[d, b],
-            recv_sem=in_recv.at[back, b],
+            src_ref=src,
+            dst_ref=halo_in.at[back, b, part],
+            send_sem=edge_send.at[d, b, part],
+            recv_sem=in_recv.at[back, b, part],
             device_id=at(1, dr, dc),
             device_id_type=MESH,
         )
 
-    def main_copy(b, part):
-        span = pl.ds(part * half, half)
+    def extent(section, part):
+        cut = half - section
+        return (0, cut) if part == 0 else (cut, height)
+
+    def main_copy(b, part, section):
+        y0, y1 = extent(section, part)
+        span = pl.ds(y0, y1 - y0)
         return pltpu.make_async_remote_copy(
             src_ref=new_hidden.at[b, span],
             dst_ref=main_in.at[b, span],
@@ -189,6 +212,10 @@
             device_id_type=MESH,
         )
 
+    def in_part(d, part):
+        dr = AROUND[d][0]
+        return dr == 0 or (dr < 0) == (part == 0)
+
     for b in range(batch):
         for d, (dr, dc) in enumerate(AROUND):
 
@@ -200,28 +227,39 @@
             def _():
                 lat_copy(d, b).start()
 
-    def convolved(main, halo, w):
-        left, right = PAD - 1, PAD + width
-        wide[1 : height + 1, PAD : PAD + width, :] = main.astype(F32)
+    left, right = PAD - 1, PAD + width
+
+    def put_side(dc, y0, y1, strip):
+        side = left if dc < 0 else right
+        wide[1 + y0 : 1 + y1, side : side + 1, :] = strip.reshape(y1 - y0, 1, chans)
+
+    def put_line(dr, dc, strip):
+        y = 0 if dr < 0 else height + 1
+        if dc == 0:
+            wide[y, PAD : PAD + width, :] = strip
+        elif dc < 0:
+            wide[y, left : left + 1, :] = strip[width - 1 : width]
+        else:
+            wide[y, right : right + 1, :] = strip[0:1]
+
+    def put_all(source, halo, b):
+        for y in range(height):
+            wide[1 + y, PAD : PAD + width, :] = source[b, line(y)].astype(F32)
         for d, (dr, dc) in enumerate(AROUND):
-            strip = halo(d).astype(F32)
-            line = 0 if dr < 0 else height + 1
+            strip = halo[d, b].astype(F32)
             if dr == 0:
-                side = left if dc < 0 else right
-                wide[1 : height + 1, side : side + 1, :] = strip.reshape(height, 1, chans)
-            elif dc == 0:
-                wide[line, PAD : PAD + width, :] = strip
-            elif dc < 0:
-                wide[line, left : left + 1, :] = strip[width - 1 : width]
+                put_side(dc, 0, height, strip)
             else:
-                wide[line, right : right + 1, :] = strip[0:1]
+                put_line(dr, dc, strip)
+
+    def convolved(y0, y1, w):
         for dx in range(3):
-            taps[:, :, dx * chans : (dx + 1) * chans] = wide[
-                :, left + dx : left + dx + width, :
+            taps[y0 : y1 + 2, :, dx * chans : (dx + 1) * chans] = wide[
+                y0 : y1 + 2, left + dx : left + dx + width, :
             ].astype(BF16)
         patch = jnp.concatenate(
             [
-                taps[dy : dy + height].reshape(height * width, 3 * chans)
+                taps[y0 + dy : y1 + dy].reshape((y1 - y0) * width, 3 * chans)
                 for dy in range(3)
             ],
             axis=-1,
@@ -237,62 +275,103 @@
                 own_copy(opposite(d), b).wait_recv()
 
         if b == 0:
-            loads[2].wait()
-        gates[...] = convolved(hidden[b], lambda d: halo_own[d, b], w_own) + bias_ref[...]
-
-        @pl.when(first)
-        def _():
-            main_in[b] = latent[b]
-
-        for d, (dr, dc) in enumerate(AROUND):
-
-            @pl.when(inside(dr, dc))
-            def _():
-                edge_copy(opposite(d), b).wait_recv()
+            for load in loads[2:5]:
+                load.wait()
+        put_all(hidden, halo_own, b)
+        gates[...] = convolved(0, height, w_own) + bias_ref[...]
 
         for part in range(2):
+            if part == 0:
+
+                @pl.when(first)
+                def _():
+                    for d, (dr, dc) in enumerate(AROUND):
+
+                        @pl.when(inside(dr, dc))
+                        def _():
+                            lat_copy(opposite(d), b).wait_recv()
+
+                    put_all(latent, halo_lat, b)
+
+            y0, y1 = (0, half) if part == 0 else (least, height)
 
             @pl.when(s > 0)
             def _():
-                main_copy(b, part).wait_recv()
-
-        if b == 0:
-            loads[3].wait()
-        gates[...] += convolved(main_in[b], lambda d: halo_in[d, b], w_in)
-        if b == 0:
-            loads[4].wait()
-
-            @pl.when(feeds)
-            def _():
-                pl.semaphore_wait(ready, listeners)
-
-        for part in range(2):
-            span = pl.ds(part * half, half)
-            z = gates[part * half * width : (part + 1) * half * width]
-            old = cell[b, span].reshape(half * width, chans)
+                for d, (dr, dc) in enumerate(AROUND):
+                    if in_part(d, part):
+
+                        @pl.when(inside(dr, dc))
+                        def _():
+                            edge_copy(opposite(d), b, part).wait_recv()
+
+                        strip = halo_in[d, b, part].astype(F32)
+                        if dr == 0:
+                            put_side(dc, y0, y1, strip[: y1 - y0])
+                        else:
+                            put_line(dr, dc, strip)
+
+            for section in range(1, sections):
+
+                @pl.when(s == section)
+                def _():
+                    main_copy(b, part, section - 1).wait_recv()
+                    m0, m1 = extent(section - 1, part)
+                    wide[1 + m0 : 1 + m1, PAD : PAD + width, :] = main_in[b, m0:m1].astype(F32)
+
+            if b == 0 and part == 0:
+                for load in loads[5:8]:
+                    load.wait()
+            z = gates[y0 * width : y1 * width] + convolved(y0, y1, w_in)
+            if b == 0 and part == 0:
+                loads[8].wait()
+            count = (y1 - y0) * width
+            old = ordered(cell, b, y0, y1).reshape(count, chans)
             gate_i = sigmoid(z[:, :chans])
             gate_f = sigmoid(z[:, chans : 2 * chans])
             gate_g = jnp.tanh(z[:, 2 * chans : 3 * chans])
             gate_o = sigmoid(z[:, 3 * chans :])
             now = gate_f * old + gate_i * gate_g
-            new_cell[b, span] = now.reshape(half, width, chans)
-            out = (gate_o * jnp.tanh(now)).astype(BF16).reshape(half, width, chans)
-            new_hidden[b, span] = out
+            out = (gate_o * jnp.tanh(now)).astype(BF16).reshape(y1 - y0, width, chans)
+            now = now.reshape(y1 - y0, width, chans)
+
+            for y in range(y0, y1):
+                if part == 0 or y >= half:
+                    new_hidden[b, y] = out[y - y0]
+                else:
+
+                    @pl.when(y >= half - s)
+                    def _():
+                        new_hidden[b, y] = out[y - y0]
+
             tile = out.astype(F32)
-            new_edges[0, b, span] = tile[:, 0, :].astype(BF16)
-            new_edges[1, b, span] = tile[:, width - 1, :].astype(BF16)
+            spare = jnp.zeros((height - (y1 - y0), chans), F32)
+            for side, x in enumerate((0, width - 1)):
+                new_edges[side, b, part] = jnp.concatenate([tile[:, x, :], spare]).astype(BF16)
+
+            if b == 0 and part == 0:
+
+                @pl.when(feeds)
+                def _():
+                    pl.semaphore_wait(ready, listeners)
+
+            for section in range(sections - 1):
+
+                @pl.when(s == section)
+                def _():
+                    main_copy(b, part, section).start()
+
             for d, (dr, dc) in enumerate(AROUND):
-                if (part == 0) == (dr < 0):
+                if in_part(d, part):
 
                     @pl.when(inside(dr, dc) & feeds)
                     def _():
-                        edge_copy(d, b).start()
-
-            @pl.when(feeds)
-            def _():
-                main_copy(b, part).start()
-
-        for k, (src, dst) in enumerate(((new_cell, cell_out), (new_hidden, hidden_out))):
+                        edge_copy(d, b, part).start()
+
+            for y in range(y0, y1):
+                new_cell[b, line(y)] = now[y - y0]
+                out_hidden[b, line(y)] = out[y - y0]
+
+        for k, (src, dst) in enumerate(((new_cell, cell_out), (out_hidden, hidden_out))):
             store = pltpu.make_async_copy(src.at[b], dst.at[0, b], store_sem.at[k, b])
             store.start()
             stores.append(store)
@@ -308,15 +387,19 @@
             def _():
                 lat_copy(d, b).wait_send()
 
-            @pl.when(inside(dr, dc) & feeds)
-            def _():
-                edge_copy(d, b).wait_send()
+            for part in range(2):
+                if in_part(d, part):
+
+                    @pl.when(inside(dr, dc) & feeds)
+                    def _():
+                        edge_copy(d, b, part).wait_send()
 
         for part in range(2):
-
-            @pl.when(feeds)
-            def _():
-                main_copy(b, part).wait_send()
+            for section in range(sections - 1):
+
+                @pl.when(s == section)
+                def _():
+                    main_copy(b, part, section).wait_send()
 
     for store in stores:
         store.wait()
@@ -328,7 +411,7 @@
     gate_chans = weights.shape[-1]
     around = len(AROUND)
     edge = max(height, width)
-    assert height == width and height % 16 == 0
+    assert height == width and height % 16 == 0 and sizes[0] < height // 2
     tile = (batch, height, width, chans)
     dma = pltpu.SemaphoreType.DMA
     anywhere = pl.BlockSpec(memory_space=pltpu.HBM)
@@ -348,23 +431,26 @@
             pltpu.VMEM((9, chans, gate_chans), BF16),
             pltpu.VMEM((9, chans, gate_chans), BF16),
             pltpu.VMEM(tile, BF16),
+            pltpu.VMEM((around, batch, 2, edge, chans), BF16),
             pltpu.VMEM((around, batch, edge, chans), BF16),
             pltpu.VMEM((around, batch, edge, chans), BF16),
             pltpu.VMEM((2, batch, edge, chans), BF16),
             pltpu.VMEM((2, batch, edge, chans), BF16),
-            pltpu.VMEM((2, batch, edge, chans), BF16),
+            pltpu.VMEM((2, batch, 2, edge, chans), BF16),
+            pltpu.VMEM(tile, BF16),
             pltpu.VMEM(tile, BF16),
             pltpu.VMEM(tile, F32),
             pltpu.VMEM((height + 2, width + 2 * PAD, chans), F32),
             pltpu.VMEM((height + 2, width, 3 * chans), BF16),
             pltpu.VMEM((height * width, gate_chans), F32),
-            dma((5,)),
+            dma((9,)),
             dma((2, batch)),
             dma((around, batch)),
             dma((around, batch)),
             dma((around, batch)),
             dma((around, batch)),
-            dma((around, batch)),
+            dma((around, batch, 2)),
+            dma((around, batch, 2)),
             dma((batch, 2)),
             dma((batch, 2)),
             pltpu.SemaphoreType.REGULAR,

time: 27.7 us -> 27.5 us (level)
  no operation moved by 1% of the time
where the time goes in v3:
time: 27.5 us; the launch traced here: 27.2 us
  Pallas kernels  23.3 us (85%)
  local copies, waits for them, and re-layouts  3.24 us (12%)
  between operations  0.64 us (2%)
    pallas_call x1, Pallas kernels, on_device(): pl.pallas_call(functools.partial(kernel, sizes), out_shape=(jax.ShapeDtyp...  23.3 us
    unnamed x2, local copies, waits for them, and re-layouts  3.24 us

profile of v3, /device:TPU:7, one launch (start us, length us, event | category | flops | bytes accessed | tf_op | source)
XLA Modules:
  0.0 27.2 jit_solution(12000444649874156897)
XLA Ops:
  0.6 23.3 %shard_map.68 = (bf16[1,2,16,16,128]{4,3,2,1,0:T(8,128)(2,1)}, f32[1,2,16,16,128]{4,3,2,1,0:T(8,128)}) custom-call(bf16[2,16,16,128]{3,2,1,0:T(8,128)(2,1)} %latent_hbm.1, bf16[1,2,16,16,128]{4,3,2,1,0:T(8,128)(2,1)} %hidden_hbm.1, f32[1,2,16,16,128]{4,3,2,1,0:T(8,128)} %cell_hbm.1, bf16[1,9,256,512]{3,2,1,0:T(8,128)(2,1)} %weights_hbm.1, f32[1,512]{1,0:T(1,128)} %bias_ref.1), custom_call_target="tpu_custom_call" | custom-call | flops 1207959552 | bytes 2359296 | tf_op jit(solution)/shard_map/pallas_call | solution.py:419
  23.9 1.6 %copy.9 = bf16[1,2,16,16,128]{4,3,2,1,0:T(8,128)(2,1)} copy(bf16[1,2,16,16,128]{4,3,2,1,0:T(8,128)(2,1)} %get-tuple-element.4) | data formatting | bytes 262144
  25.5 1.7 %copy.10 = f32[1,2,16,16,128]{4,3,2,1,0:T(8,128)} copy(f32[1,2,16,16,128]{4,3,2,1,0:T(8,128)} %get-tuple-element.5) | data formatting | bytes 524288

commit v4 on v3

--- a/solution.py
+++ b/solution.py
@@ -10,13 +10,13 @@
 MESH = pl.DeviceIdType.MESH
 F32 = jnp.float32
 BF16 = jnp.bfloat16
-AROUND = tuple((dr, dc) for dr in (-1, 0, 1) for dc in (-1, 0, 1) if (dr, dc) != (0, 0))
 PAD = 8
 
 
-def opposite(d):
-    dr, dc = AROUND[d]
-    return AROUND.index((dr, -dc))
+def directions(sizes):
+    across = (-1, 0, 1) if sizes[1] > 2 else (0, 1) if sizes[1] > 1 else (0,)
+    along = (-1, 0, 1) if sizes[2] > 1 else (0,)
+    return tuple((dr, dc) for dr in across for dc in along if (dr, dc) != (0, 0))
 
 
 def sigmoid(x):
@@ -30,8 +30,9 @@
     cell_hbm,
     weights_hbm,
     bias_ref,
-    hidden_out,
-    cell_out,
+    kept_out,
+    added_out,
+    opened_out,
     latent,
     hidden,
     cell,
@@ -39,14 +40,17 @@
     w_own,
     main_in,
     halo_in,
+    corner_in,
+    new_corners,
     halo_own,
     halo_lat,
     own_edges,
     lat_edges,
     new_edges,
     new_hidden,
-    out_hidden,
-    new_cell,
+    kept,
+    added,
+    opened,
     wide,
     taps,
     gates,
@@ -62,6 +66,7 @@
     main_recv,
     ready,
 ):
+    around = directions(sizes)
     sections, rows, cols = sizes
     batch, height, width, chans = latent.shape
     half = height // 2
@@ -80,6 +85,10 @@
     def ordered(source, b, y0, y1):
         return jnp.stack([source[b, line(y)] for y in range(y0, y1)])
 
+    def opposite(d):
+        dr, dc = around[d]
+        return around.index((dr, -dc))
+
     def inside(dr, dc):
         return (r + dr * step >= 0) & (r + dr * step < rows) & (c + dc >= 0) & (c + dc < cols)
 
@@ -102,13 +111,15 @@
         load.start()
 
     halo_in[...] = jnp.zeros_like(halo_in)
+    corner_in[...] = jnp.zeros_like(corner_in)
     halo_own[...] = jnp.zeros_like(halo_own)
+    wide[...] = jnp.zeros_like(wide)
     halo_lat[...] = jnp.zeros_like(halo_lat)
 
     barrier = pltpu.get_barrier_semaphore()
     expected = jnp.int32(0)
     listeners = jnp.int32(0)
-    for dr, dc in AROUND + ((0, 0),):
+    for dr, dc in around + ((0, 0),):
         there = inside(dr, dc)
         if (dr, dc) != (0, 0):
 
@@ -118,7 +129,7 @@
 
             expected = expected + there.astype(jnp.int32)
 
-    for dr, dc in AROUND + ((0, 0),):
+    for dr, dc in around + ((0, 0),):
         there = inside(dr, dc)
 
         @pl.when(there & feeds)
@@ -145,51 +156,53 @@
 
     pl.semaphore_wait(barrier, expected)
 
-    for dr, dc in AROUND + ((0, 0),):
+    for dr, dc in around + ((0, 0),):
 
         @pl.when(inside(dr, dc) & (s > 0))
         def _():
             pl.semaphore_signal(ready, inc=1, device_id=at(-1, dr, dc), device_id_type=MESH)
 
-    def edge(tile, edges, b, dr, dc):
+    def edge(tile, edges, dr, dc):
         if dr == 0:
-            return edges.at[0 if dc < 0 else 1, b]
-        return tile.at[b, line(0 if dr < 0 else height - 1)]
-
-    def own_copy(d, b):
-        dr, dc = AROUND[d]
+            return edges.at[0 if dc < 0 else 1]
+        return tile.at[:, line(0 if dr < 0 else height - 1)]
+
+    def own_copy(d):
+        dr, dc = around[d]
         back = opposite(d)
         return pltpu.make_async_remote_copy(
-            src_ref=edge(hidden, own_edges, b, dr, dc),
-            dst_ref=halo_own.at[back, b],
-            send_sem=own_send.at[d, b],
-            recv_sem=own_recv.at[back, b],
+            src_ref=edge(hidden, own_edges, dr, dc),
+            dst_ref=halo_own.at[back],
+            send_sem=own_send.at[d],
+            recv_sem=own_recv.at[back],
             device_id=at(0, dr, dc),
             device_id_type=MESH,
         )
 
-    def lat_copy(d, b):
-        dr, dc = AROUND[d]
+    def lat_copy(d):
+        dr, dc = around[d]
         back = opposite(d)
         return pltpu.make_async_remote_copy(
-            src_ref=edge(latent, lat_edges, b, dr, dc),
-            dst_ref=halo_lat.at[back, b],
-            send_sem=lat_send.at[d, b],
-            recv_sem=lat_recv.at[back, b],
+            src_ref=edge(latent, lat_edges, dr, dc),
+            dst_ref=halo_lat.at[back],
+            send_sem=lat_send.at[d],
+            recv_sem=lat_recv.at[back],
             device_id=at(0, dr, dc),
             device_id_type=MESH,
         )
 
     def edge_copy(d, b, part):
-        dr, dc = AROUND[d]
+        dr, dc = around[d]
         back = opposite(d)
         if dr == 0:
-            src = new_edges.at[0 if dc < 0 else 1, b, part]
+            src, dst = new_edges.at[0 if dc < 0 else 1, b, part], halo_in.at[back, b, part]
+        elif dc == 0:
+            src, dst = new_hidden.at[b, 0 if dr < 0 else height - 1], halo_in.at[back, b, part]
         else:
-            src = new_hidden.at[b, 0 if dr < 0 else height - 1]
+            src, dst = new_corners.at[0 if dc < 0 else 1, b, part], corner_in.at[back, b]
         return pltpu.make_async_remote_copy(
             src_ref=src,
-            dst_ref=halo_in.at[back, b, part],
+            dst_ref=dst,
             send_sem=edge_send.at[d, b, part],
             recv_sem=in_recv.at[back, b, part],
             device_id=at(1, dr, dc),
@@ -213,19 +226,20 @@
         )
 
     def in_part(d, part):
-        dr = AROUND[d][0]
+        dr = around[d][0]
         return dr == 0 or (dr < 0) == (part == 0)
 
-    for b in range(batch):
-        for d, (dr, dc) in enumerate(AROUND):
-
-            @pl.when(inside(dr, dc))
-            def _():
-                own_copy(d, b).start()
-
-            @pl.when(inside(dr, dc) & first)
-            def _():
-                lat_copy(d, b).start()
+    for d, (dr, dc) in enumerate(around):
+
+        @pl.when(inside(dr, dc) & first)
+        def _():
+            lat_copy(d).start()
+
+    for d, (dr, dc) in enumerate(around):
+
+        @pl.when(inside(dr, dc))
+        def _():
+            own_copy(d).start()
 
     left, right = PAD - 1, PAD + width
 
@@ -245,7 +259,7 @@
     def put_all(source, halo, b):
         for y in range(height):
             wide[1 + y, PAD : PAD + width, :] = source[b, line(y)].astype(F32)
-        for d, (dr, dc) in enumerate(AROUND):
+        for d, (dr, dc) in enumerate(around):
             strip = halo[d, b].astype(F32)
             if dr == 0:
                 put_side(dc, 0, height, strip)
@@ -268,13 +282,13 @@
 
     stores = []
     for b in range(batch):
-        for d, (dr, dc) in enumerate(AROUND):
-
-            @pl.when(inside(dr, dc))
-            def _():
-                own_copy(opposite(d), b).wait_recv()
-
         if b == 0:
+            for d, (dr, dc) in enumerate(around):
+
+                @pl.when(inside(dr, dc))
+                def _():
+                    own_copy(opposite(d)).wait_recv()
+
             for load in loads[2:5]:
                 load.wait()
         put_all(hidden, halo_own, b)
@@ -285,11 +299,12 @@
 
                 @pl.when(first)
                 def _():
-                    for d, (dr, dc) in enumerate(AROUND):
-
-                        @pl.when(inside(dr, dc))
-                        def _():
-                            lat_copy(opposite(d), b).wait_recv()
+                    if b == 0:
+                        for d, (dr, dc) in enumerate(around):
+
+                            @pl.when(inside(dr, dc))
+                            def _():
+                                lat_copy(opposite(d)).wait_recv()
 
                     put_all(latent, halo_lat, b)
 
@@ -297,18 +312,21 @@
 
             @pl.when(s > 0)
             def _():
-                for d, (dr, dc) in enumerate(AROUND):
+                for d, (dr, dc) in enumerate(around):
                     if in_part(d, part):
 
                         @pl.when(inside(dr, dc))
                         def _():
                             edge_copy(opposite(d), b, part).wait_recv()
 
-                        strip = halo_in[d, b, part].astype(F32)
                         if dr == 0:
+                            strip = halo_in[d, b, part].astype(F32)
                             put_side(dc, y0, y1, strip[: y1 - y0])
+                        elif dc == 0:
+                            put_line(dr, dc, halo_in[d, b, part].astype(F32))
                         else:
-                            put_line(dr, dc, strip)
+                            y, side = 0 if dr < 0 else height + 1, left if dc < 0 else right
+                            wide[y, side : side + 1, :] = corner_in[d, b]
 
             for section in range(1, sections):
 
@@ -330,9 +348,9 @@
             gate_f = sigmoid(z[:, chans : 2 * chans])
             gate_g = jnp.tanh(z[:, 2 * chans : 3 * chans])
             gate_o = sigmoid(z[:, 3 * chans :])
-            now = gate_f * old + gate_i * gate_g
+            keep, add = gate_f * old, gate_i * gate_g
+            now = keep + add
             out = (gate_o * jnp.tanh(now)).astype(BF16).reshape(y1 - y0, width, chans)
-            now = now.reshape(y1 - y0, width, chans)
 
             for y in range(y0, y1):
                 if part == 0 or y >= half:
@@ -347,6 +365,8 @@
             spare = jnp.zeros((height - (y1 - y0), chans), F32)
             for side, x in enumerate((0, width - 1)):
                 new_edges[side, b, part] = jnp.concatenate([tile[:, x, :], spare]).astype(BF16)
+                y = 0 if part == 0 else y1 - y0 - 1
+                new_corners[side, b, part] = tile[y, x : x + 1, :]
 
             if b == 0 and part == 0:
 
@@ -360,33 +380,37 @@
                 def _():
                     main_copy(b, part, section).start()
 
-            for d, (dr, dc) in enumerate(AROUND):
+            for d, (dr, dc) in enumerate(around):
                 if in_part(d, part):
 
                     @pl.when(inside(dr, dc) & feeds)
                     def _():
                         edge_copy(d, b, part).start()
 
-            for y in range(y0, y1):
-                new_cell[b, line(y)] = now[y - y0]
-                out_hidden[b, line(y)] = out[y - y0]
-
-        for k, (src, dst) in enumerate(((new_cell, cell_out), (out_hidden, hidden_out))):
+            for value, ref in ((keep, kept), (add, added), (gate_o, opened)):
+                value = value.reshape(y1 - y0, width, chans)
+                for y in range(y0, y1):
+                    ref[b, line(y)] = value[y - y0]
+
+        for k, (src, dst) in enumerate(
+            ((kept, kept_out), (added, added_out), (opened, opened_out))
+        ):
             store = pltpu.make_async_copy(src.at[b], dst.at[0, b], store_sem.at[k, b])
             store.start()
             stores.append(store)
 
+    for d, (dr, dc) in enumerate(around):
+
+        @pl.when(inside(dr, dc))
+        def _():
+            own_copy(d).wait_send()
+
+        @pl.when(inside(dr, dc) & first)
+        def _():
+            lat_copy(d).wait_send()
+
     for b in range(batch):
-        for d, (dr, dc) in enumerate(AROUND):
-
-            @pl.when(inside(dr, dc))
-            def _():
-                own_copy(d, b).wait_send()
-
-            @pl.when(inside(dr, dc) & first)
-            def _():
-                lat_copy(d, b).wait_send()
-
+        for d, (dr, dc) in enumerate(around):
             for part in range(2):
                 if in_part(d, part):
 
@@ -409,21 +433,18 @@
     sizes = tuple(lax.axis_size(axis) for axis in ("section", "row", "col"))
     batch, height, width, chans = latent.shape
     gate_chans = weights.shape[-1]
-    around = len(AROUND)
+    around = len(directions(sizes))
     edge = max(height, width)
     assert height == width and height % 16 == 0 and sizes[0] < height // 2
     tile = (batch, height, width, chans)
     dma = pltpu.SemaphoreType.DMA
     anywhere = pl.BlockSpec(memory_space=pltpu.HBM)
     flops = 2 * batch * height * width * 9 * 2 * chans * gate_chans
-    return pl.pallas_call(
+    kept, added, opened = pl.pallas_call(
         functools.partial(kernel, sizes),
-        out_shape=(
-            jax.ShapeDtypeStruct(hidden_old.shape, BF16),
-            jax.ShapeDtypeStruct(cell_old.shape, F32),
-        ),
+        out_shape=(jax.ShapeDtypeStruct(cell_old.shape, F32),) * 3,
         in_specs=[anywhere] * 4 + [pl.BlockSpec(memory_space=pltpu.VMEM)],
-        out_specs=(anywhere, anywhere),
+        out_specs=(anywhere,) * 3,
         scratch_shapes=[
             pltpu.VMEM(tile, BF16),
             pltpu.VMEM(tile, BF16),
@@ -432,23 +453,26 @@
             pltpu.VMEM((9, chans, gate_chans), BF16),
             pltpu.VMEM(tile, BF16),
             pltpu.VMEM((around, batch, 2, edge, chans), BF16),
+            pltpu.VMEM((around, batch, 1, chans), F32),
+            pltpu.VMEM((2, batch, 2, 1, chans), F32),
             pltpu.VMEM((around, batch, edge, chans), BF16),
             pltpu.VMEM((around, batch, edge, chans), BF16),
             pltpu.VMEM((2, batch, edge, chans), BF16),
             pltpu.VMEM((2, batch, edge, chans), BF16),
             pltpu.VMEM((2, batch, 2, edge, chans), BF16),
             pltpu.VMEM(tile, BF16),
-            pltpu.VMEM(tile, BF16),
+            pltpu.VMEM(tile, F32),
+            pltpu.VMEM(tile, F32),
             pltpu.VMEM(tile, F32),
             pltpu.VMEM((height + 2, width + 2 * PAD, chans), F32),
             pltpu.VMEM((height + 2, width, 3 * chans), BF16),
             pltpu.VMEM((height * width, gate_chans), F32),
             dma((9,)),
-            dma((2, batch)),
-            dma((around, batch)),
-            dma((around, batch)),
-            dma((around, batch)),
-            dma((around, batch)),
+            dma((3, batch)),
+            dma((around,)),
+            dma((around,)),
+            dma((around,)),
+            dma((around,)),
             dma((around, batch, 2)),
             dma((around, batch, 2)),
             dma((batch, 2)),
@@ -462,6 +486,8 @@
             flops=flops, bytes_accessed=weights.size * 2, transcendentals=0
         ),
     )(latent, hidden_old, cell_old, weights, bias)
+    cell = kept + added
+    return (opened * jnp.tanh(cell)).astype(BF16), cell
 
 
 def solution(mesh):

time: 27.5 us -> 25 us (0.909)
  local copies, waits for them, and re-layouts: 3.24 us -> 0 us
  other arithmetic: 0 us -> 1.9 us
  Pallas kernels: 23.3 us -> 22.3 us
    unnamed x2 -> x0, local copies, waits for them, and re-layouts: 3.24 us -> none
    convert_element_type x0 -> x1, other arithmetic: none -> 1.9 us  [on_device(): return ((opened * jnp.tanh(cell)).astype(BF16), cell)]
    pallas_call x1, Pallas kernels: 23.3 us -> 22.3 us  [on_device(): pl.pallas_call(functools.partial(kernel, sizes), out_shape=(jax.ShapeDtyp...]
where the time goes in v4:
time: 25 us; the launch traced here: 24.9 us
  Pallas kernels  22.3 us (89%)
  other arithmetic  1.9 us (8%)
  between operations  0.64 us (3%)
    pallas_call x1, Pallas kernels, on_device(): pl.pallas_call(functools.partial(kernel, sizes), out_shape=(jax.ShapeDtyp...  22.3 us
    convert_element_type x1, other arithmetic, on_device(): return ((opened * jnp.tanh(cell)).astype(BF16), cell)  1.9 us

profile of v4, /device:TPU:7, one launch (start us, length us, event | category | flops | bytes accessed | tf_op | source)
XLA Modules:
  0.0 24.9 jit_solution(4531415680547048514)
XLA Ops:
  0.6 22.3 %shard_map.68 = (f32[1,2,16,16,128]{4,3,2,1,0:T(8,128)}, f32[1,2,16,16,128]{4,3,2,1,0:T(8,128)}, f32[1,2,16,16,128]{4,3,2,1,0:T(8,128)}) custom-call(bf16[2,16,16,128]{3,2,1,0:T(8,128)(2,1)} %latent_hbm.1, bf16[1,2,16,16,128]{4,3,2,1,0:T(8,128)(2,1)} %hidden_hbm.1, f32[1,2,16,16,128]{4,3,2,1,0:T(8,128)} %cell_hbm.1, bf16[1,9,256,512]{3,2,1,0:T(8,128)(2,1)} %weights_hbm.1, ...), custom_call_target="tpu_custom_call" | custom-call | flops 1207959552 | bytes 2359296 | tf_op jit(solution)/shard_map/pallas_call | solution.py:443
  23.0 1.9 %multiply_convert_fusion = (bf16[1,2,16,16,128]{4,3,2,1,0:T(8,128)(2,1)}, f32[1,2,16,16,128]{4,3,2,1,0:T(8,128)}) fusion(f32[1,2,16,16,128]{4,3,2,1,0:T(8,128)} %get-tuple-element.5, f32[1,2,16,16,128]{4,3,2,1,0:T(8,128)} %get-tuple-element.6, f32[1,2,16,16,128]{4,3,2,1,0:T(8,128)} %get-tuple-element.7), kind=kLoop, calls=%fused_computation | loop fusion | flops 196608 | bytes 1179648 | tf_op jit(solution)/shard_map/convert_element_type | solution.py:490

commit v5 on v4

--- a/solution.py
+++ b/solution.py
@@ -53,7 +53,9 @@
     opened,
     wide,
     taps,
+    border,
     gates,
+    total,
     load_sem,
     store_sem,
     own_send,
@@ -247,24 +249,12 @@
         side = left if dc < 0 else right
         wide[1 + y0 : 1 + y1, side : side + 1, :] = strip.reshape(y1 - y0, 1, chans)
 
-    def put_line(dr, dc, strip):
-        y = 0 if dr < 0 else height + 1
-        if dc == 0:
-            wide[y, PAD : PAD + width, :] = strip
-        elif dc < 0:
-            wide[y, left : left + 1, :] = strip[width - 1 : width]
-        else:
-            wide[y, right : right + 1, :] = strip[0:1]
-
-    def put_all(source, halo, b):
+    def put_line(dr, strip):
+        wide[0 if dr < 0 else height + 1, PAD : PAD + width, :] = strip
+
+    def put_tile(source, b):
         for y in range(height):
             wide[1 + y, PAD : PAD + width, :] = source[b, line(y)].astype(F32)
-        for d, (dr, dc) in enumerate(around):
-            strip = halo[d, b].astype(F32)
-            if dr == 0:
-                put_side(dc, 0, height, strip)
-            else:
-                put_line(dr, dc, strip)
 
     def convolved(y0, y1, w):
         for dx in range(3):
@@ -280,34 +270,73 @@
         )
         return jnp.dot(patch, w[...].reshape(9 * chans, -1), preferred_element_type=F32)
 
+    def add_borders(halo, w):
+        side_cells = height
+        for d, (dr, dc) in enumerate(around):
+            if dr != 0 and dc != 0:
+                continue
+            border[:, PAD : PAD + side_cells, :] = halo[d].astype(F32)
+            for end, place in ((-1, PAD - 1), (1, PAD + side_cells)):
+                if dr == 0 and (end, dc) in around:
+                    x = width - 1 if dc < 0 else 0
+                    corner = halo[around.index((end, dc))].astype(F32)[:, x : x + 1, :]
+                else:
+                    corner = jnp.zeros((batch, 1, chans), F32)
+                border[:, place : place + 1, :] = corner
+            patch = jnp.concatenate(
+                [
+                    border[:, PAD - 1 + k : PAD - 1 + k + side_cells, :].reshape(-1, chans)
+                    for k in range(3)
+                ],
+                axis=-1,
+            ).astype(BF16)
+            if dr == 0:
+                part_w = jnp.concatenate([w[3 * k + 1 + dc] for k in range(3)], axis=0)
+            else:
+                part_w = w[3 + 3 * dr : 6 + 3 * dr].reshape(3 * chans, -1)
+            more = jnp.dot(patch, part_w, preferred_element_type=F32)
+            more = more.reshape(batch, side_cells, -1)
+            if dr == 0:
+                x = 0 if dc < 0 else width - 1
+                for b in range(batch):
+                    gates[b, :, x, :] += more[b]
+            else:
+                gates[:, 0 if dr < 0 else height - 1] += more
+
+    for load in loads[2:5]:
+        load.wait()
+    for b in range(batch):
+        put_tile(hidden, b)
+        gates[b] = (convolved(0, height, w_own) + bias_ref[...]).reshape(height, width, -1)
+    for load in loads[5:8]:
+        load.wait()
+
+    @pl.when(first)
+    def _():
+        for b in range(batch):
+            put_tile(latent, b)
+            gates[b] += convolved(0, height, w_in).reshape(height, width, -1)
+
+        for d, (dr, dc) in enumerate(around):
+
+            @pl.when(inside(dr, dc))
+            def _():
+                lat_copy(opposite(d)).wait_recv()
+
+        add_borders(halo_lat, w_in)
+
+    for d, (dr, dc) in enumerate(around):
+
+        @pl.when(inside(dr, dc))
+        def _():
+            own_copy(opposite(d)).wait_recv()
+
+    add_borders(halo_own, w_own)
+    loads[8].wait()
+
     stores = []
     for b in range(batch):
-        if b == 0:
-            for d, (dr, dc) in enumerate(around):
-
-                @pl.when(inside(dr, dc))
-                def _():
-                    own_copy(opposite(d)).wait_recv()
-
-            for load in loads[2:5]:
-                load.wait()
-        put_all(hidden, halo_own, b)
-        gates[...] = convolved(0, height, w_own) + bias_ref[...]
-
         for part in range(2):
-            if part == 0:
-
-                @pl.when(first)
-                def _():
-                    if b == 0:
-                        for d, (dr, dc) in enumerate(around):
-
-                            @pl.when(inside(dr, dc))
-                            def _():
-                                lat_copy(opposite(d)).wait_recv()
-
-                    put_all(latent, halo_lat, b)
-
             y0, y1 = (0, half) if part == 0 else (least, height)
 
             @pl.when(s > 0)
@@ -323,7 +352,7 @@
                             strip = halo_in[d, b, part].astype(F32)
                             put_side(dc, y0, y1, strip[: y1 - y0])
                         elif dc == 0:
-                            put_line(dr, dc, halo_in[d, b, part].astype(F32))
+                            put_line(dr, halo_in[d, b, part].astype(F32))
                         else:
                             y, side = 0 if dr < 0 else height + 1, left if dc < 0 else right
                             wide[y, side : side + 1, :] = corner_in[d, b]
@@ -336,13 +365,17 @@
                     m0, m1 = extent(section - 1, part)
                     wide[1 + m0 : 1 + m1, PAD : PAD + width, :] = main_in[b, m0:m1].astype(F32)
 
-            if b == 0 and part == 0:
-                for load in loads[5:8]:
-                    load.wait()
-            z = gates[y0 * width : y1 * width] + convolved(y0, y1, w_in)
-            if b == 0 and part == 0:
-                loads[8].wait()
             count = (y1 - y0) * width
+
+            @pl.when(first)
+            def _():
+                total[:count] = gates[b, y0:y1].reshape(count, -1)
+
+            @pl.when(s > 0)
+            def _():
+                total[:count] = gates[b, y0:y1].reshape(count, -1) + convolved(y0, y1, w_in)
+
+            z = total[:count]
             old = ordered(cell, b, y0, y1).reshape(count, chans)
             gate_i = sigmoid(z[:, :chans])
             gate_f = sigmoid(z[:, chans : 2 * chans])
@@ -466,6 +499,8 @@
             pltpu.VMEM(tile, F32),
             pltpu.VMEM((height + 2, width + 2 * PAD, chans), F32),
             pltpu.VMEM((height + 2, width, 3 * chans), BF16),
+            pltpu.VMEM((batch, edge + 2 * PAD, chans), F32),
+            pltpu.VMEM((batch, height, width, gate_chans), F32),
             pltpu.VMEM((height * width, gate_chans), F32),
             dma((9,)),
             dma((3, batch)),

time: 25 us -> 24.8 us (level)
  Pallas kernels: 22.3 us -> 22 us
    pallas_call x1, Pallas kernels: 22.3 us -> 22 us  [on_device(): pl.pallas_call(functools.partial(kernel, sizes), out_shape=(jax.ShapeDtyp...]
where the time goes in v5:
time: 24.8 us; the launch traced here: 24.6 us
  Pallas kernels  22 us (89%)
  other arithmetic  1.9 us (8%)
  between operations  0.64 us (3%)
    pallas_call x1, Pallas kernels, on_device(): pl.pallas_call(functools.partial(kernel, sizes), out_shape=(jax.ShapeDtyp...  22 us
    convert_element_type x1, other arithmetic, on_device(): return ((opened * jnp.tanh(cell)).astype(BF16), cell)  1.9 us

profile of v5, /device:TPU:7, one launch (start us, length us, event | category | flops | bytes accessed | tf_op | source)
XLA Modules:
  0.0 24.6 jit_solution(7262660116217870999)
XLA Ops:
  0.6 22.0 %shard_map.68 = (f32[1,2,16,16,128]{4,3,2,1,0:T(8,128)}, f32[1,2,16,16,128]{4,3,2,1,0:T(8,128)}, f32[1,2,16,16,128]{4,3,2,1,0:T(8,128)}) custom-call(bf16[2,16,16,128]{3,2,1,0:T(8,128)(2,1)} %latent_hbm.1, bf16[1,2,16,16,128]{4,3,2,1,0:T(8,128)(2,1)} %hidden_hbm.1, f32[1,2,16,16,128]{4,3,2,1,0:T(8,128)} %cell_hbm.1, bf16[1,9,256,512]{3,2,1,0:T(8,128)(2,1)} %weights_hbm.1, ...), custom_call_target="tpu_custom_call" | custom-call | flops 1207959552 | bytes 2359296 | tf_op jit(solution)/shard_map/pallas_call | solution.py:476
  22.7 1.9 %multiply_convert_fusion = (bf16[1,2,16,16,128]{4,3,2,1,0:T(8,128)(2,1)}, f32[1,2,16,16,128]{4,3,2,1,0:T(8,128)}) fusion(f32[1,2,16,16,128]{4,3,2,1,0:T(8,128)} %get-tuple-element.5, f32[1,2,16,16,128]{4,3,2,1,0:T(8,128)} %get-tuple-element.6, f32[1,2,16,16,128]{4,3,2,1,0:T(8,128)} %get-tuple-element.7), kind=kLoop, calls=%fused_computation | loop fusion | flops 196608 | bytes 1179648 | tf_op jit(solution)/shard_map/convert_element_type | solution.py:525

commit v6 on v5

--- a/solution.py
+++ b/solution.py
@@ -71,7 +71,7 @@
     around = directions(sizes)
     sections, rows, cols = sizes
     batch, height, width, chans = latent.shape
-    half = height // 2
+    half = height * 5 // 8
     least = half - (sections - 1)
     s = lax.axis_index("section")
     r = lax.axis_index("row")
@@ -109,7 +109,7 @@
             + [(cell_hbm.at[0], cell)]
         )
     ]
-    for load in loads:
+    for load in loads[:2]:
         load.start()
 
     halo_in[...] = jnp.zeros_like(halo_in)
@@ -140,6 +140,9 @@
 
         expected = expected + (there & (s > 0)).astype(jnp.int32)
         listeners = listeners + (there & feeds).astype(jnp.int32)
+
+    for load in loads[2:]:
+        load.start()
 
     def pack(source, edges, b):
         tile = ordered(source, b, 0, height).astype(F32)
@@ -407,18 +410,18 @@
                 def _():
                     pl.semaphore_wait(ready, listeners)
 
+            for d, (dr, dc) in enumerate(around):
+                if in_part(d, part):
+
+                    @pl.when(inside(dr, dc) & feeds)
+                    def _():
+                        edge_copy(d, b, part).start()
+
             for section in range(sections - 1):
 
                 @pl.when(s == section)
                 def _():
                     main_copy(b, part, section).start()
-
-            for d, (dr, dc) in enumerate(around):
-                if in_part(d, part):
-
-                    @pl.when(inside(dr, dc) & feeds)
-                    def _():
-                        edge_copy(d, b, part).start()
 
             for value, ref in ((keep, kept), (add, added), (gate_o, opened)):
                 value = value.reshape(y1 - y0, width, chans)

time: 24.8 us -> 24.6 us (level)
  no operation moved by 1% of the time
where the time goes in v6:
time: 24.6 us; the launch traced here: 24.4 us
  Pallas kernels  21.9 us (89%)
  other arithmetic  1.9 us (8%)
  between operations  0.64 us (3%)
    pallas_call x1, Pallas kernels, on_device(): pl.pallas_call(functools.partial(kernel, sizes), out_shape=(jax.ShapeDtyp...  21.9 us
    convert_element_type x1, other arithmetic, on_device(): return ((opened * jnp.tanh(cell)).astype(BF16), cell)  1.9 us

profile of v6, /device:TPU:7, one launch (start us, length us, event | category | flops | bytes accessed | tf_op | source)
XLA Modules:
  0.0 24.4 jit_solution(5955103535901490004)
XLA Ops:
  0.6 21.9 %shard_map.68 = (f32[1,2,16,16,128]{4,3,2,1,0:T(8,128)}, f32[1,2,16,16,128]{4,3,2,1,0:T(8,128)}, f32[1,2,16,16,128]{4,3,2,1,0:T(8,128)}) custom-call(bf16[2,16,16,128]{3,2,1,0:T(8,128)(2,1)} %latent_hbm.1, bf16[1,2,16,16,128]{4,3,2,1,0:T(8,128)(2,1)} %hidden_hbm.1, f32[1,2,16,16,128]{4,3,2,1,0:T(8,128)} %cell_hbm.1, bf16[1,9,256,512]{3,2,1,0:T(8,128)(2,1)} %weights_hbm.1, ...), custom_call_target="tpu_custom_call" | custom-call | flops 1207959552 | bytes 2359296 | tf_op jit(solution)/shard_map/pallas_call | solution.py:479
  22.5 1.9 %multiply_convert_fusion = (bf16[1,2,16,16,128]{4,3,2,1,0:T(8,128)(2,1)}, f32[1,2,16,16,128]{4,3,2,1,0:T(8,128)}) fusion(f32[1,2,16,16,128]{4,3,2,1,0:T(8,128)} %get-tuple-element.5, f32[1,2,16,16,128]{4,3,2,1,0:T(8,128)} %get-tuple-element.6, f32[1,2,16,16,128]{4,3,2,1,0:T(8,128)} %get-tuple-element.7), kind=kLoop, calls=%fused_computation | loop fusion | flops 196608 | bytes 1179648 | tf_op jit(solution)/shard_map/convert_element_type | solution.py:528

commit v7 on v6

--- a/solution.py
+++ b/solution.py
@@ -39,6 +39,7 @@
     w_in,
     w_own,
     main_in,
+    passing,
     halo_in,
     corner_in,
     new_corners,
@@ -66,6 +67,8 @@
     edge_send,
     main_send,
     main_recv,
+    relay_send,
+    relay_recv,
     ready,
 ):
     around = directions(sizes)
@@ -77,6 +80,8 @@
     r = lax.axis_index("row")
     c = lax.axis_index("col")
     first = s == 0
+    relays = sections > 3
+    origin, relay = relays & (s == 1), relays & (s == 3)
     feeds = s + 1 < sections
     odd = lax.rem(r, 2)
     step = 1 - 2 * odd
@@ -141,6 +146,13 @@
         expected = expected + (there & (s > 0)).astype(jnp.int32)
         listeners = listeners + (there & feeds).astype(jnp.int32)
 
+    @pl.when(origin)
+    def _():
+        pl.semaphore_signal(barrier, inc=1, device_id=at(2, 0, 0), device_id_type=MESH)
+
+    expected = expected + relay.astype(jnp.int32)
+    listeners = listeners + origin.astype(jnp.int32)
+
     for load in loads[2:]:
         load.start()
 
@@ -166,6 +178,10 @@
         @pl.when(inside(dr, dc) & (s > 0))
         def _():
             pl.semaphore_signal(ready, inc=1, device_id=at(-1, dr, dc), device_id_type=MESH)
+
+    @pl.when(relay)
+    def _():
+        pl.semaphore_signal(ready, inc=1, device_id=at(-2, 0, 0), device_id_type=MESH)
 
     def edge(tile, edges, dr, dc):
         if dr == 0:
@@ -218,8 +234,27 @@
         cut = half - section
         return (0, cut) if part == 0 else (cut, height)
 
+    def middle(part):
+        y0, y1 = extent(1, part)
+        return y0 + (y1 - y0) * 2 // 5
+
+    def relay_copy(b, part, leg):
+        y0 = extent(1, part)[0]
+        span = pl.ds(y0, middle(part) - y0)
+        src, dst = ((new_hidden, passing), (passing, main_in))[leg]
+        return pltpu.make_async_remote_copy(
+            src_ref=src.at[b, span],
+            dst_ref=dst.at[b, span],
+            send_sem=relay_send.at[leg, b, part],
+            recv_sem=relay_recv.at[leg, b, part],
+            device_id=at(2 if leg == 0 else -1, 0, 0),
+            device_id_type=MESH,
+        )
+
     def main_copy(b, part, section):
         y0, y1 = extent(section, part)
+        if relays and section == 1:
+            y0 = middle(part)
         span = pl.ds(y0, y1 - y0)
         return pltpu.make_async_remote_copy(
             src_ref=new_hidden.at[b, span],
@@ -337,6 +372,15 @@
     add_borders(halo_own, w_own)
     loads[8].wait()
 
+    if relays:
+
+        @pl.when(relay)
+        def _():
+            for b in range(batch):
+                for part in range(2):
+                    relay_copy(b, part, 0).wait_recv()
+                    relay_copy(b, part, 1).start()
+
     stores = []
     for b in range(batch):
         for part in range(2):
@@ -365,6 +409,8 @@
                 @pl.when(s == section)
                 def _():
                     main_copy(b, part, section - 1).wait_recv()
+                    if relays and section == 2:
+                        relay_copy(b, part, 1).wait_recv()
                     m0, m1 = extent(section - 1, part)
                     wide[1 + m0 : 1 + m1, PAD : PAD + width, :] = main_in[b, m0:m1].astype(F32)
 
@@ -421,6 +467,8 @@
 
                 @pl.when(s == section)
                 def _():
+                    if relays and section == 1:
+                        relay_copy(b, part, 0).start()
                     main_copy(b, part, section).start()
 
             for value, ref in ((keep, kept), (add, added), (gate_o, opened)):
@@ -460,6 +508,16 @@
                 @pl.when(s == section)
                 def _():
                     main_copy(b, part, section).wait_send()
+                    if relays and section == 1:
+                        relay_copy(b, part, 0).wait_send()
+
+    if relays:
+
+        @pl.when(relay)
+        def _():
+            for b in range(batch):
+                for part in range(2):
+                    relay_copy(b, part, 1).wait_send()
 
     for store in stores:
         store.wait()
@@ -487,6 +545,7 @@
             pltpu.VMEM(tile, F32),
             pltpu.VMEM((9, chans, gate_chans), BF16),
             pltpu.VMEM((9, chans, gate_chans), BF16),
+            pltpu.VMEM(tile, BF16),
             pltpu.VMEM(tile, BF16),
             pltpu.VMEM((around, batch, 2, edge, chans), BF16),
             pltpu.VMEM((around, batch, 1, chans), F32),
@@ -515,6 +574,8 @@
             dma((around, batch, 2)),
             dma((batch, 2)),
             dma((batch, 2)),
+            dma((2, batch, 2)),
+            dma((2, batch, 2)),
             pltpu.SemaphoreType.REGULAR,
         ],
         compiler_params=pltpu.CompilerParams(

time: 24.6 us -> 26.2 us (1.065)
  Pallas kernels: 21.9 us -> 23.5 us
    pallas_call x1, Pallas kernels: 21.9 us -> 23.5 us  [on_device(): pl.pallas_call(functools.partial(kernel, sizes), out_shape=(jax.ShapeDtyp...]
where the time goes in v7:
time: 26.2 us; the launch traced here: 26 us
  Pallas kernels  23.5 us (90%)
  other arithmetic  1.9 us (7%)
  between operations  0.64 us (2%)
    pallas_call x1, Pallas kernels, on_device(): pl.pallas_call(functools.partial(kernel, sizes), out_shape=(jax.ShapeDtyp...  23.5 us
    convert_element_type x1, other arithmetic, on_device(): return ((opened * jnp.tanh(cell)).astype(BF16), cell)  1.9 us

profile of v7, /device:TPU:7, one launch (start us, length us, event | category | flops | bytes accessed | tf_op | source)
XLA Modules:
  0.0 26.0 jit_solution(2162574841698869635)
XLA Ops:
  0.6 23.5 %shard_map.68 = (f32[1,2,16,16,128]{4,3,2,1,0:T(8,128)}, f32[1,2,16,16,128]{4,3,2,1,0:T(8,128)}, f32[1,2,16,16,128]{4,3,2,1,0:T(8,128)}) custom-call(bf16[2,16,16,128]{3,2,1,0:T(8,128)(2,1)} %latent_hbm.1, bf16[1,2,16,16,128]{4,3,2,1,0:T(8,128)(2,1)} %hidden_hbm.1, f32[1,2,16,16,128]{4,3,2,1,0:T(8,128)} %cell_hbm.1, bf16[1,9,256,512]{3,2,1,0:T(8,128)(2,1)} %weights_hbm.1, ...), custom_call_target="tpu_custom_call" | custom-call | flops 1207959552 | bytes 2359296 | tf_op jit(solution)/shard_map/pallas_call | solution.py:537
  24.1 1.9 %multiply_convert_fusion = (bf16[1,2,16,16,128]{4,3,2,1,0:T(8,128)(2,1)}, f32[1,2,16,16,128]{4,3,2,1,0:T(8,128)}) fusion(f32[1,2,16,16,128]{4,3,2,1,0:T(8,128)} %get-tuple-element.5, f32[1,2,16,16,128]{4,3,2,1,0:T(8,128)} %get-tuple-element.6, f32[1,2,16,16,128]{4,3,2,1,0:T(8,128)} %get-tuple-element.7), kind=kLoop, calls=%fused_computation | loop fusion | flops 196608 | bytes 1179648 | tf_op jit(solution)/shard_map/convert_element_type | solution.py:589

commit v8 on v6

--- a/solution.py
+++ b/solution.py
@@ -308,17 +308,29 @@
 
     for load in loads[2:5]:
         load.wait()
-    for b in range(batch):
+    gates[...] = jnp.broadcast_to(bias_ref[...].reshape(1, 1, 1, -1), gates.shape)
+
+    def add_own(b):
         put_tile(hidden, b)
-        gates[b] = (convolved(0, height, w_own) + bias_ref[...]).reshape(height, width, -1)
+        gates[b] += convolved(0, height, w_own).reshape(height, width, -1)
+
+    def add_latent(b):
+        put_tile(latent, b)
+        gates[b] += convolved(0, height, w_in).reshape(height, width, -1)
+
+    add_own(0)
+
+    @pl.when(s > 0)
+    def _():
+        for b in range(1, batch):
+            add_own(b)
+
     for load in loads[5:8]:
         load.wait()
 
     @pl.when(first)
     def _():
-        for b in range(batch):
-            put_tile(latent, b)
-            gates[b] += convolved(0, height, w_in).reshape(height, width, -1)
+        add_latent(0)
 
         for d, (dr, dc) in enumerate(around):
 
@@ -339,6 +351,13 @@
 
     stores = []
     for b in range(batch):
+        if b > 0:
+
+            @pl.when(first)
+            def _():
+                add_own(b)
+                add_latent(b)
+
         for part in range(2):
             y0, y1 = (0, half) if part == 0 else (least, height)
 

time: 24.6 us -> 24.5 us (level)
  no operation moved by 1% of the time
where the time goes in v8:
time: 24.5 us; the launch traced here: 24.3 us
  Pallas kernels  21.8 us (89%)
  other arithmetic  1.9 us (8%)
  between operations  0.64 us (3%)
    pallas_call x1, Pallas kernels, on_device(): pl.pallas_call(functools.partial(kernel, sizes), out_shape=(jax.ShapeDtyp...  21.8 us
    convert_element_type x1, other arithmetic, on_device(): return ((opened * jnp.tanh(cell)).astype(BF16), cell)  1.9 us

profile of v8, /device:TPU:7, one launch (start us, length us, event | category | flops | bytes accessed | tf_op | source)
XLA Modules:
  0.0 24.3 jit_solution(4869995005529731531)
XLA Ops:
  0.6 21.8 %shard_map.68 = (f32[1,2,16,16,128]{4,3,2,1,0:T(8,128)}, f32[1,2,16,16,128]{4,3,2,1,0:T(8,128)}, f32[1,2,16,16,128]{4,3,2,1,0:T(8,128)}) custom-call(bf16[2,16,16,128]{3,2,1,0:T(8,128)(2,1)} %latent_hbm.1, bf16[1,2,16,16,128]{4,3,2,1,0:T(8,128)(2,1)} %hidden_hbm.1, f32[1,2,16,16,128]{4,3,2,1,0:T(8,128)} %cell_hbm.1, bf16[1,9,256,512]{3,2,1,0:T(8,128)(2,1)} %weights_hbm.1, ...), custom_call_target="tpu_custom_call" | custom-call | flops 1207959552 | bytes 2359296 | tf_op jit(solution)/shard_map/pallas_call | solution.py:498
  22.4 1.9 %multiply_convert_fusion = (bf16[1,2,16,16,128]{4,3,2,1,0:T(8,128)(2,1)}, f32[1,2,16,16,128]{4,3,2,1,0:T(8,128)}) fusion(f32[1,2,16,16,128]{4,3,2,1,0:T(8,128)} %get-tuple-element.5, f32[1,2,16,16,128]{4,3,2,1,0:T(8,128)} %get-tuple-element.6, f32[1,2,16,16,128]{4,3,2,1,0:T(8,128)} %get-tuple-element.7), kind=kLoop, calls=%fused_computation | loop fusion | flops 196608 | bytes 1179648 | tf_op jit(solution)/shard_map/convert_element_type | solution.py:547
